TPU v7x, 32 devices: a whole 2x2x4 slice. The times are simulated.
32 devices in a mesh: seq: 16 (over z, y, core), col: 2 (over x).
Axes of the slice: x: 2, y: 2, z: 4, core: 2. Of those that a mesh axis runs over, the one named last changes fastest.
Arguments:
- tokens: int32 [2, 16, 512], P(None, 'seq', 'col'), may hold values from 4 to 28
- targets: int32 [2, 16, 512], P(None, 'seq', 'col'), may hold values from 4 to 28
- masked: int32 [2, 16, 512], P(None, 'seq', 'col'), may hold values from 0 to 1, as said below
- contact_pairs: int32 [2, 2048, 2], P(None, ('seq', 'col')), may hold values from 0 to 511, as said below
- labels: int32 [2, 2048], P(None, ('seq', 'col')), may hold values from -1 to 1, as said below
- attention_in_master: float32 [2, 768, 2304], P(None, ('seq', 'col')), may hold values from -0.21875 to 0.21875
- attention_in_first: float32 [2, 768, 2304], P(None, ('seq', 'col')), may hold values from -2.0861626e-07 to 2.0861626e-07
- attention_in_second: float32 [2, 768, 2304], P(None, ('seq', 'col')), may hold values from 5.2805643e-15 to 2.1122257e-14
- attention_out_master: float32 [2, 768, 768], P(None, ('seq', 'col')), may hold values from -1.75 to 1.75
- attention_out_first: float32 [2, 768, 768], P(None, ('seq', 'col')), may hold values from -2.0861626e-07 to 2.0861626e-07
- attention_out_second: float32 [2, 768, 768], P(None, ('seq', 'col')), may hold values from 5.2805643e-15 to 2.1122257e-14
- feed_up_master: float32 [768, 3072], P(('seq', 'col')), may hold values from -0.21875 to 0.21875
- feed_up_first: float32 [768, 3072], P(('seq', 'col')), may hold values from -2.0861626e-07 to 2.0861626e-07
- feed_up_second: float32 [768, 3072], P(('seq', 'col')), may hold values from 5.2805643e-15 to 2.1122257e-14
- feed_down_master: float32 [3072, 768], P(None, ('seq', 'col')), may hold values from -0.109375 to 0.109375
- feed_down_first: float32 [3072, 768], P(None, ('seq', 'col')), may hold values from -2.0861626e-07 to 2.0861626e-07
- feed_down_second: float32 [3072, 768], P(None, ('seq', 'col')), may hold values from 5.2805643e-15 to 2.1122257e-14
- embedding_master: float32 [33, 768], P(None, ('seq', 'col')), may hold values from -6 to 6
- embedding_first: float32 [33, 768], P(None, ('seq', 'col')), may hold values from -8.34465e-07 to 8.34465e-07
- embedding_second: float32 [33, 768], P(None, ('seq', 'col')), may hold values from 8.448903e-14 to 3.3795612e-13
- norm_params_master: float32 [8, 768], P(None, ('seq', 'col'))
- norm_params_first: float32 [8, 768], P(None, ('seq', 'col')), may hold values from -8.34465e-07 to 8.34465e-07
- norm_params_second: float32 [8, 768], P(None, ('seq', 'col')), may hold values from 8.448903e-14 to 3.3795612e-13
- contact_head_master: float32 [13], replicated, may hold values from -6 to 6
- contact_head_first: float32 [13], replicated, may hold values from -2.2888184e-05 to 2.2888184e-05
- contact_head_second: float32 [13], replicated, may hold values from 3.1683386e-12 to 1.26733546e-11
Outputs:
- attention_in_new: float32 [2, 768, 2304], P(None, ('seq', 'col'))
- attention_in_moment: float32 [2, 768, 2304], P(None, ('seq', 'col'))
- attention_in_square: float32 [2, 768, 2304], P(None, ('seq', 'col'))
- attention_out_new: float32 [2, 768, 768], P(None, ('seq', 'col'))
- attention_out_moment: float32 [2, 768, 768], P(None, ('seq', 'col'))
- attention_out_square: float32 [2, 768, 768], P(None, ('seq', 'col'))
- feed_up_new: float32 [768, 3072], P(('seq', 'col'))
- feed_up_moment: float32 [768, 3072], P(('seq', 'col'))
- feed_up_square: float32 [768, 3072], P(('seq', 'col'))
- feed_down_new: float32 [3072, 768], P(None, ('seq', 'col'))
- feed_down_moment: float32 [3072, 768], P(None, ('seq', 'col'))
- feed_down_square: float32 [3072, 768], P(None, ('seq', 'col'))
- embedding_new: float32 [33, 768], P(None, ('seq', 'col'))
- embedding_moment: float32 [33, 768], P(None, ('seq', 'col'))
- embedding_square: float32 [33, 768], P(None, ('seq', 'col'))
- norm_params_new: float32 [8, 768], P(None, ('seq', 'col'))
- norm_params_moment: float32 [8, 768], P(None, ('seq', 'col'))
- norm_params_square: float32 [8, 768], P(None, ('seq', 'col'))
- contact_head_new: float32 [13], replicated
- contact_head_moment: float32 [13], replicated
- contact_head_square: float32 [13], replicated
- attention_in_copy: bfloat16 [2, 768, 2304], P(None, ('seq', 'col'))
- attention_out_copy: bfloat16 [2, 768, 768], P(None, ('seq', 'col'))
- feed_up_copy: bfloat16 [768, 3072], P(('seq', 'col'))
- feed_down_copy: bfloat16 [3072, 768], P(None, ('seq', 'col'))
- embedding_copy: bfloat16 [33, 768], P(None, ('seq', 'col'))
- loss_parts: float32 [4], replicated
- grad_norm: float32 [], replicated
Inputs may be any that keep to these rules, and one draw needn't show every extreme that they name: 1 marks a masked residue. `contact_pairs`: pairs are laid out in blocks of 64, one block for each shard of the seq+col axes; the first column of a pair lies among the 256 columns of its shard's col index. `labels`: -1: pair ignored; 1: contact; 0: no contact.
All inputs are finite; a program needn't handle non-finite values.
Results may differ from a plain program's by a relative error of at most 0.0081.
The roundings to bfloat16 on the way count: a program that leaves them out, or rounds other values in their place, can miss the bound.
Values may be sent and summed in bfloat16 or wider, within the bound.
A program may use at most 320 MiB of HBM per device.

v0:
```python
import jax
import jax.numpy as jnp
from jax import lax
from jax.sharding import PartitionSpec as P

D = 768
HEADS = 12
HD = 64
FF = 3072
VOCAB = 33
C = 512
STEP = 10


PRECISE = lax.Precision.HIGHEST
NORM_EPS = 1e-05
MASK_ID = 32
MAX_NORM = 0.001
LEARN_RATE = 0.05
VECTOR_RATE = 0.5
BETA_ONE = 0.9
BETA_TWO = 0.95
ADAM_EPS = 1e-08
WEIGHT_DECAY = 0.01


def layer_norm(values, scale_vec, shift_vec):
    centre = values - jnp.mean(values, -1, keepdims=True)
    spread = jnp.mean(centre * centre, -1, keepdims=True)
    return centre * lax.rsqrt(spread + NORM_EPS) * scale_vec + shift_vec


def norm_back(values, scale_vec, shift_vec, upstream):
    unused, pullback = jax.vjp(layer_norm, values, scale_vec, shift_vec)
    return pullback(upstream)


def matmul(left, right):
    return jnp.dot(left, right, preferred_element_type=jnp.float32)


def matmul_left(left, right):
    return lax.dot_general(
        left, right, (((0,), (0,)), ((), ())), preferred_element_type=jnp.float32
    )


def matmul_right(left, right):
    return lax.dot_general(
        left, right, (((1,), (1,)), ((), ())), preferred_element_type=jnp.float32
    )


def softmax_back(probability, upstream):
    return probability * (upstream - jnp.sum(probability * upstream, -1, keepdims=True))


def split_heads(block):
    return block.reshape(block.shape[0], block.shape[1], HEADS, HD)


def forward(
    weights, contact_head, inputs, targets, masked, contact_pairs, labels, counts, col_base
):
    attention_in, attention_out, feed_up, feed_down, table, norm_params = weights
    rows, cols = inputs.shape
    tokens_here = rows * cols
    row_scale = (HD * rows * lax.axis_size("seq")) ** (-0.5)
    norms = norm_params.astype(jnp.float32)
    one_hot = (inputs.reshape(tokens_here, 1) == jnp.arange(VOCAB)[None, :]).astype(jnp.float32)
    embedded = matmul(one_hot.astype(jnp.bfloat16), table)
    row_normed = layer_norm(embedded, norms[0], norms[4]).astype(jnp.bfloat16)
    row_proj = matmul(row_normed, attention_in[0]).astype(jnp.bfloat16).reshape(rows, cols, 3 * D)
    row_query = split_heads(row_proj[..., :D])
    row_pair = lax.all_gather(row_proj[..., D:], "col", axis=1, tiled=True)
    partial_score = (
        jnp.einsum(
            "rihe,rjhe->ihj",
            row_query,
            split_heads(row_pair[..., :D]),
            preferred_element_type=jnp.float32,
        )
        * row_scale
    )
    score_share = lax.psum_scatter(
        partial_score.reshape(cols * HEADS, C), "seq", scatter_dimension=0, tiled=True
    )
    prob_share = jax.nn.softmax(score_share, axis=-1)
    row_prob = lax.all_gather(prob_share.astype(jnp.bfloat16), "seq", axis=0, tiled=True).reshape(
        cols, HEADS, C
    )
    row_mixed = (
        jnp.einsum(
            "ihj,rjhe->rihe",
            row_prob,
            split_heads(row_pair[..., D:]),
            preferred_element_type=jnp.float32,
        )
        .astype(jnp.bfloat16)
        .reshape(tokens_here, D)
    )
    after_row = embedded + matmul(row_mixed, attention_out[0])
    local_query = contact_pairs[:, 0] - col_base
    features = row_prob[local_query, :, contact_pairs[:, 1]].astype(jnp.float32)
    contact_logit = (
        jnp.dot(features, contact_head[:HEADS], precision=PRECISE) * C + contact_head[HEADS]
    )
    positive = (labels == 1).astype(jnp.float32)
    valid = labels >= 0
    bce_sum = jnp.sum(
        jnp.where(valid, jax.nn.softplus(contact_logit) - positive * contact_logit, 0.0)
    )
    contact_coef = jnp.where(valid, jax.nn.sigmoid(contact_logit) - positive, 0.0) / counts[1]
    col_normed = layer_norm(after_row, norms[1], norms[5]).astype(jnp.bfloat16)
    col_proj = matmul(col_normed, attention_in[1]).astype(jnp.bfloat16).reshape(rows, cols, 3 * D)
    col_query = split_heads(col_proj[..., :D])
    col_pair = lax.all_gather(col_proj[..., D:], "seq", axis=0, tiled=True)
    col_score = jnp.einsum(
        "rche,sche->chrs",
        col_query,
        split_heads(col_pair[..., :D]),
        preferred_element_type=jnp.float32,
    ) * HD ** (-0.5)
    col_prob = jax.nn.softmax(col_score, axis=-1)
    col_prob_low = col_prob.astype(jnp.bfloat16)
    col_mixed = (
        jnp.einsum(
            "chrs,sche->rche",
            col_prob_low,
            split_heads(col_pair[..., D:]),
            preferred_element_type=jnp.float32,
        )
        .astype(jnp.bfloat16)
        .reshape(tokens_here, D)
    )
    col_state = (col_query, col_pair, col_prob, col_prob_low)
    after_col = after_row + matmul(col_mixed, attention_out[1])
    feed_normed = layer_norm(after_col, norms[2], norms[6]).astype(jnp.bfloat16)
    hidden_up = matmul(feed_normed, feed_up)
    active = jax.nn.gelu(hidden_up).astype(jnp.bfloat16)
    after_feed = after_col + matmul(active, feed_down)
    head_normed = layer_norm(after_feed, norms[3], norms[7]).astype(jnp.bfloat16)
    logits = matmul_right(head_normed, table) * D ** (-0.5)
    log_probs = jax.nn.log_softmax(logits, axis=-1)
    target_hot = (targets.reshape(tokens_here, 1) == jnp.arange(VOCAB)[None, :]).astype(jnp.float32)
    keep_cell = masked.reshape(tokens_here, 1) > 0
    mlm_sum = -jnp.sum(jnp.where(keep_cell, target_hot * log_probs, 0.0))
    logit_grad = jnp.where(keep_cell, jnp.exp(log_probs) - target_hot, 0.0) / counts[0]
    saved = (
        one_hot,
        embedded,
        after_row,
        after_col,
        after_feed,
        row_normed,
        row_query,
        row_pair,
        prob_share,
        row_prob,
        row_mixed,
        col_normed,
        col_state,
        col_mixed,
        feed_normed,
        hidden_up,
        active,
        head_normed,
        features,
        local_query,
        contact_coef,
        logit_grad,
    )
    return (saved, mlm_sum, bce_sum)


def backward(weights, contact_head, saved, contact_pairs):
    attention_in, attention_out, feed_up, feed_down, table, norm_params = weights
    (
        one_hot,
        embedded,
        after_row,
        after_col,
        after_feed,
        row_normed,
        row_query,
        row_pair,
        prob_share,
        row_prob,
        row_mixed,
        col_normed,
        col_state,
        col_mixed,
        feed_normed,
        hidden_up,
        active,
        head_normed,
        features,
        local_query,
        contact_coef,
        logit_grad,
    ) = saved
    rows, cols = (row_query.shape[0], row_query.shape[1])
    tokens_here = rows * cols
    all_rows = rows * lax.axis_size("seq")
    row_scale = (HD * all_rows) ** (-0.5)
    norms = norm_params.astype(jnp.float32)
    logit_low = (logit_grad * D ** (-0.5)).astype(jnp.bfloat16)
    grad_table = matmul_left(logit_low, head_normed)
    grad_stream, scale_three, shift_three = norm_back(
        after_feed, norms[3], norms[7], matmul(logit_low, table)
    )
    branch_low = grad_stream.astype(jnp.bfloat16)
    grad_down = matmul_left(active, branch_low)
    unused, gelu_pull = jax.vjp(jax.nn.gelu, hidden_up)
    (grad_up,) = gelu_pull(matmul_right(branch_low, feed_down))
    up_low = grad_up.astype(jnp.bfloat16)
    grad_feed_up = matmul_left(feed_normed, up_low)
    grad_inner, scale_two, shift_two = norm_back(
        after_col, norms[2], norms[6], matmul_right(up_low, feed_up)
    )
    grad_stream = grad_stream + grad_inner
    branch_low = grad_stream.astype(jnp.bfloat16)
    grad_out_col = matmul_left(col_mixed, branch_low)
    mixed_low = matmul_right(branch_low, attention_out[1]).astype(jnp.bfloat16)
    col_query, col_pair, col_prob, col_prob_low = col_state
    mixed_heads = mixed_low.reshape(rows, cols, HEADS, HD)
    col_key = split_heads(col_pair[..., :D])
    col_value = split_heads(col_pair[..., D:])
    prob_grad = jnp.einsum(
        "rche,sche->chrs", mixed_heads, col_value, preferred_element_type=jnp.float32
    )
    score_low = softmax_back(col_prob, prob_grad).astype(jnp.bfloat16)
    grad_query = jnp.einsum(
        "chrs,sche->rche", score_low, col_key, preferred_element_type=jnp.float32
    ) * HD ** (-0.5)
    grad_key = jnp.einsum(
        "chrs,rche->sche", score_low, col_query, preferred_element_type=jnp.float32
    ) * HD ** (-0.5)
    grad_value = jnp.einsum(
        "chrs,rche->sche", col_prob_low, mixed_heads, preferred_element_type=jnp.float32
    )
    grad_pair = lax.psum_scatter(
        jnp.concatenate(
            [grad_key.reshape(all_rows, cols, D), grad_value.reshape(all_rows, cols, D)], -1
        ).astype(jnp.bfloat16),
        "seq",
        scatter_dimension=0,
        tiled=True,
    ).astype(jnp.float32)
    proj_low = (
        jnp.concatenate([grad_query.reshape(rows, cols, D), grad_pair], -1)
        .astype(jnp.bfloat16)
        .reshape(tokens_here, 3 * D)
    )
    grad_in_col = matmul_left(col_normed, proj_low)
    grad_inner, scale_one, shift_one = norm_back(
        after_row, norms[1], norms[5], matmul_right(proj_low, attention_in[1])
    )
    grad_stream = grad_stream + grad_inner
    branch_low = grad_stream.astype(jnp.bfloat16)
    grad_out_row = matmul_left(row_mixed, branch_low)
    mixed_low = (
        matmul_right(branch_low, attention_out[0])
        .astype(jnp.bfloat16)
        .reshape(rows, cols, HEADS, HD)
    )
    row_key = split_heads(row_pair[..., :D])
    row_value = split_heads(row_pair[..., D:])
    partial_grad = jnp.einsum(
        "rihe,rjhe->ihj", mixed_low, row_value, preferred_element_type=jnp.float32
    )
    partial_grad = partial_grad.at[local_query, :, contact_pairs[:, 1]].add(
        contact_coef[:, None] * contact_head[None, :HEADS] * C
    )
    grad_contact = jnp.concatenate(
        [jnp.dot(contact_coef, features, precision=PRECISE) * C, jnp.sum(contact_coef)[None]]
    )
    grad_share = lax.psum_scatter(
        partial_grad.reshape(cols * HEADS, C), "seq", scatter_dimension=0, tiled=True
    )
    share_low = softmax_back(prob_share, grad_share).astype(jnp.bfloat16)
    score_low = lax.all_gather(share_low, "seq", axis=0, tiled=True).reshape(cols, HEADS, C)
    grad_query = (
        jnp.einsum("ihj,rjhe->rihe", score_low, row_key, preferred_element_type=jnp.float32)
        * row_scale
    )
    grad_key = (
        jnp.einsum("ihj,rihe->rjhe", score_low, row_query, preferred_element_type=jnp.float32)
        * row_scale
    )
    grad_value = jnp.einsum(
        "ihj,rihe->rjhe", row_prob, mixed_low, preferred_element_type=jnp.float32
    )
    grad_pair = lax.psum_scatter(
        jnp.concatenate([grad_key.reshape(rows, C, D), grad_value.reshape(rows, C, D)], -1),
        "col",
        scatter_dimension=1,
        tiled=True,
    )
    proj_low = (
        jnp.concatenate([grad_query.reshape(rows, cols, D), grad_pair], -1)
        .astype(jnp.bfloat16)
        .reshape(tokens_here, 3 * D)
    )
    grad_in_row = matmul_left(row_normed, proj_low)
    grad_inner, scale_zero, shift_zero = norm_back(
        embedded, norms[0], norms[4], matmul_right(proj_low, attention_in[0])
    )
    grad_stream = grad_stream + grad_inner
    grad_table = grad_table + jnp.einsum("nv,nd->vd", one_hot, grad_stream, precision=PRECISE)
    grads = (
        jnp.stack([grad_in_row, grad_in_col]),
        jnp.stack([grad_out_row, grad_out_col]),
        grad_feed_up,
        grad_down,
        grad_table,
        jnp.stack(
            [
                scale_zero,
                scale_one,
                scale_two,
                scale_three,
                shift_zero,
                shift_one,
                shift_two,
                shift_three,
            ]
        ),
    )
    return (grads, grad_contact)


def adam_update(master, first, second, grad_part, rate):
    first = BETA_ONE * first + (1.0 - BETA_ONE) * grad_part
    second = BETA_TWO * second + (1.0 - BETA_TWO) * grad_part * grad_part
    moved = first / (1.0 - BETA_ONE**STEP) / (jnp.sqrt(second / (1.0 - BETA_TWO**STEP)) + ADAM_EPS)
    return (master - rate * (moved + WEIGHT_DECAY * master), first, second)


def shards(
    tokens,
    targets,
    masked,
    contact_pairs,
    labels,
    attention_in_master,
    attention_in_first,
    attention_in_second,
    attention_out_master,
    attention_out_first,
    attention_out_second,
    feed_up_master,
    feed_up_first,
    feed_up_second,
    feed_down_master,
    feed_down_first,
    feed_down_second,
    embedding_master,
    embedding_first,
    embedding_second,
    norm_params_master,
    norm_params_first,
    norm_params_second,
    contact_head_master,
    contact_head_first,
    contact_head_second,
):
    micro_count = tokens.shape[0]
    col_base = lax.axis_index("col") * tokens.shape[2]
    counts = lax.psum(
        (jnp.sum(masked).astype(jnp.float32), jnp.sum(labels >= 0).astype(jnp.float32)),
        ("seq", "col"),
    )
    inputs_all = jnp.where(masked > 0, MASK_ID, tokens)
    casts = (
        attention_in_master.astype(jnp.bfloat16),
        attention_out_master.astype(jnp.bfloat16),
        feed_up_master.astype(jnp.bfloat16),
        feed_down_master.astype(jnp.bfloat16),
        embedding_master.astype(jnp.bfloat16),
        norm_params_master.astype(jnp.bfloat16),
    )
    gathered = (
        lax.all_gather(casts[0], ("seq", "col"), axis=1, tiled=True),
        lax.all_gather(casts[1], ("seq", "col"), axis=1, tiled=True),
        lax.all_gather(casts[2], ("seq", "col"), axis=0, tiled=True),
        lax.all_gather(casts[3], ("seq", "col"), axis=1, tiled=True),
        lax.all_gather(casts[4], ("seq", "col"), axis=1, tiled=True),
        lax.all_gather(casts[5], ("seq", "col"), axis=1, tiled=True),
    )
    sums = (
        jnp.zeros((2, D, 3 * D), jnp.float32),
        jnp.zeros((2, D, D), jnp.float32),
        jnp.zeros((D, FF), jnp.float32),
        jnp.zeros((FF, D), jnp.float32),
        jnp.zeros((VOCAB, D), jnp.float32),
        jnp.zeros((8, D), jnp.float32),
    )
    contact_total = jnp.zeros((HEADS + 1,), jnp.float32)
    mlm_total = jnp.zeros((), jnp.float32)
    bce_total = jnp.zeros((), jnp.float32)
    for micro_index in range(micro_count):
        saved, mlm_sum, bce_sum = forward(
            gathered,
            contact_head_master,
            inputs_all[micro_index],
            targets[micro_index],
            masked[micro_index],
            contact_pairs[micro_index],
            labels[micro_index],
            counts,
            col_base,
        )
        grads, grad_contact = backward(
            gathered, contact_head_master, saved, contact_pairs[micro_index]
        )
        sums = tuple((summed + grad_part for summed, grad_part in zip(sums, grads)))
        contact_total = contact_total + grad_contact
        mlm_total = mlm_total + mlm_sum
        bce_total = bce_total + bce_sum
    reduced = (
        lax.psum_scatter(sums[0], ("seq", "col"), scatter_dimension=1, tiled=True),
        lax.psum_scatter(sums[1], ("seq", "col"), scatter_dimension=1, tiled=True),
        lax.psum_scatter(sums[2], ("seq", "col"), scatter_dimension=0, tiled=True),
        lax.psum_scatter(sums[3], ("seq", "col"), scatter_dimension=1, tiled=True),
        lax.psum_scatter(sums[4], ("seq", "col"), scatter_dimension=1, tiled=True),
        lax.psum_scatter(sums[5], ("seq", "col"), scatter_dimension=1, tiled=True),
    )
    mlm_total, bce_total, contact_grad = lax.psum(
        (mlm_total, bce_total, contact_total), ("seq", "col")
    )
    local_square = sum((jnp.sum(reduced_part * reduced_part) for reduced_part in reduced))
    square = lax.psum(local_square, ("seq", "col")) + jnp.sum(contact_grad * contact_grad)
    grad_norm = jnp.sqrt(square)
    factor = jnp.minimum(1.0, MAX_NORM / grad_norm)
    in_new, in_moment, in_square = adam_update(
        attention_in_master,
        attention_in_first,
        attention_in_second,
        reduced[0] * factor,
        LEARN_RATE,
    )
    out_new, out_moment, out_square = adam_update(
        attention_out_master,
        attention_out_first,
        attention_out_second,
        reduced[1] * factor,
        LEARN_RATE,
    )
    up_new, up_moment, up_square = adam_update(
        feed_up_master, feed_up_first, feed_up_second, reduced[2] * factor, LEARN_RATE
    )
    down_new, down_moment, down_square = adam_update(
        feed_down_master, feed_down_first, feed_down_second, reduced[3] * factor, LEARN_RATE
    )
    table_new, table_moment, table_square = adam_update(
        embedding_master, embedding_first, embedding_second, reduced[4] * factor, VECTOR_RATE
    )
    norm_new, norm_moment, norm_square = adam_update(
        norm_params_master, norm_params_first, norm_params_second, reduced[5] * factor, VECTOR_RATE
    )
    head_new, head_moment, head_square = adam_update(
        contact_head_master,
        contact_head_first,
        contact_head_second,
        contact_grad * factor,
        VECTOR_RATE,
    )
    loss_parts = jnp.stack([mlm_total, counts[0], bce_total, counts[1]])
    return (
        in_new,
        in_moment,
        in_square,
        out_new,
        out_moment,
        out_square,
        up_new,
        up_moment,
        up_square,
        down_new,
        down_moment,
        down_square,
        table_new,
        table_moment,
        table_square,
        norm_new,
        norm_moment,
        norm_square,
        head_new,
        head_moment,
        head_square,
        in_new.astype(jnp.bfloat16),
        out_new.astype(jnp.bfloat16),
        up_new.astype(jnp.bfloat16),
        down_new.astype(jnp.bfloat16),
        table_new.astype(jnp.bfloat16),
        loss_parts,
        grad_norm,
    )


def solution(mesh):
    placed = (
        P(None, "seq", "col"),
        P(None, "seq", "col"),
        P(None, "seq", "col"),
        P(None, ("seq", "col"), None),
        P(None, ("seq", "col")),
        P(None, ("seq", "col"), None),
        P(None, ("seq", "col"), None),
        P(None, ("seq", "col"), None),
        P(None, ("seq", "col"), None),
        P(None, ("seq", "col"), None),
        P(None, ("seq", "col"), None),
        P(("seq", "col"), None),
        P(("seq", "col"), None),
        P(("seq", "col"), None),
        P(None, ("seq", "col")),
        P(None, ("seq", "col")),
        P(None, ("seq", "col")),
        P(None, ("seq", "col")),
        P(None, ("seq", "col")),
        P(None, ("seq", "col")),
        P(None, ("seq", "col")),
        P(None, ("seq", "col")),
        P(None, ("seq", "col")),
        P(),
        P(),
        P(),
    )
    return jax.shard_map(
        shards,
        mesh=mesh,
        in_specs=placed,
        out_specs=(
            P(None, ("seq", "col"), None),
            P(None, ("seq", "col"), None),
            P(None, ("seq", "col"), None),
            P(None, ("seq", "col"), None),
            P(None, ("seq", "col"), None),
            P(None, ("seq", "col"), None),
            P(("seq", "col"), None),
            P(("seq", "col"), None),
            P(("seq", "col"), None),
            P(None, ("seq", "col")),
            P(None, ("seq", "col")),
            P(None, ("seq", "col")),
            P(None, ("seq", "col")),
            P(None, ("seq", "col")),
            P(None, ("seq", "col")),
            P(None, ("seq", "col")),
            P(None, ("seq", "col")),
            P(None, ("seq", "col")),
            P(),
            P(),
            P(),
            P(None, ("seq", "col"), None),
            P(None, ("seq", "col"), None),
            P(("seq", "col"), None),
            P(None, ("seq", "col")),
            P(None, ("seq", "col")),
            P(),
            P(),
        ),
        check_vma=False,
    )
```

profile of v0, /device:TPU:0, one launch (start us, length us, event | category | flops | bytes accessed | tf_op | source)
XLA Modules:
  0.0 2437.2 jit_solution(13309266494711283632)
XLA Ops:
  10.4 70.8 %all-gather = bf16[32,24,8]{1,2,0:T(8,128)(2,1)S(1)} all-gather(bf16[1,24,8]{1,2,0:T(8,128)(2,1)S(1)} %convert_bitcast_fusion.2), channel_id=1, replica_groups=mesh['seq'=16,'col'=2] {'seq','col'}, dimensions={0}, use_global_device_ids=true | all-gather | bytes 12672 | tf_op jit(solution)/shard_map/all_gather | solution.py:389
  81.6 64.4 %all_gather.42 = bf16[33,768]{0,1:T(8,128)(2,1)S(1)} all-gather(bf16[33,24]{0,1:T(8,128)(2,1)S(1)} %convert_element_type.234), channel_id=1, replica_groups=mesh['seq'=16,'col'=2] {'seq','col'}, dimensions={1}, use_global_device_ids=true | all-gather | bytes 52272 | tf_op jit(solution)/shard_map/all_gather | solution.py:388
  159.0 19.0 all-gather.30.cloned.1.call-done
  228.0 67.9 %reduce-scatter.25.cloned.1.call-done = f32[192,512]{1,0:T(8,128)} async-done(((f32[3072,512]{1,0:T(8,128)}), f32[192,512]{1,0:T(8,128)}) %reduce-scatter.25.cloned.1.call-update) | async-done | bytes 393232 | tf_op jit(solution)/shard_map/reduce_scatter | solution.py:85
  300.8 83.9 %reduce-scatter.17.cloned.1.call-done = f32[192,512]{1,0:T(8,128)} async-done(((f32[3072,512]{1,0:T(8,128)}), f32[192,512]{1,0:T(8,128)}) %reduce-scatter.17.cloned.1.call-update) | async-done | bytes 393232 | tf_op jit(solution)/shard_map/reduce_scatter | solution.py:85
  389.4 42.5 %all-gather.32.cloned.1.call-done = bf16[3072,512]{1,0:T(8,128)(2,1)} async-done(((bf16[192,512]{1,0:T(8,128)(2,1)}), bf16[3072,512]{1,0:T(8,128)(2,1)}) %all-gather.32.cloned.1.call-update) | async-done | bytes 3145744 | tf_op jit(solution)/shard_map/all_gather | solution.py:89
  442.1 49.5 %all-gather.20.cloned.1.call-done = bf16[2,768,768]{2,1,0:T(8,128)(2,1)} async-done(((bf16[2,24,768]{2,1,0:T(8,128)(2,1)}), bf16[2,768,768]{2,1,0:T(8,128)(2,1)}) %all-gather.20.cloned.1.call-update) | async-done | bytes 2359312 | tf_op jit(solution)/shard_map/all_gather | solution.py:385
  503.6 34.9 %all-gather.18.cloned.1.call-done = bf16[3072,512]{1,0:T(8,128)(2,1)} async-done(((bf16[192,512]{1,0:T(8,128)(2,1)}), bf16[3072,512]{1,0:T(8,128)(2,1)}) %all-gather.18.cloned.1.call-update) | async-done | bytes 3145744 | tf_op jit(solution)/shard_map/all_gather | solution.py:89
  557.5 40.4 %all-reduce.3 = (f32[]{:T(128)}, f32[]{:T(128)}) all-reduce(f32[]{:T(128)S(6)} %convert_element_type.255, f32[]{:T(128)S(6)} %convert_element_type.266), channel_id=1, replica_groups=mesh['seq'=16,'col'=2] {'seq','col'}, use_global_device_ids=true, to_apply=%region_16.18 | all-reduce | flops 2 | bytes 16 | tf_op jit(solution)/shard_map/psum | solution.py:370
  602.1 39.7 %all-gather.34.cloned.1.call-done = bf16[16,256,1536]{2,1,0:T(8,128)(2,1)} async-done(((bf16[1,256,1536]{2,1,0:T(8,128)(2,1)}), bf16[16,256,1536]{2,1,0:T(8,128)(2,1)}) %all-gather.34.cloned.1.call-update) | async-done | bytes 12582928 | tf_op jit(solution)/shard_map/all_gather | solution.py:117
  679.1 27.8 %all-gather.24.cloned.1.call-done = bf16[768,3072]{1,0:T(8,128)(2,1)} async-done(((bf16[24,3072]{1,0:T(8,128)(2,1)}), bf16[768,3072]{1,0:T(8,128)(2,1)}) %all-gather.24.cloned.1.call-update) | async-done | bytes 4718608 | tf_op jit(solution)/shard_map/all_gather | solution.py:386
  712.6 60.3 %all-gather.26.cloned.1.call-done = bf16[3072,768]{0,1:T(8,128)(2,1)} async-done(((bf16[3072,24]{0,1:T(8,128)(2,1)}), bf16[3072,768]{0,1:T(8,128)(2,1)}) %all-gather.26.cloned.1.call-update) | async-done | bytes 4718608 | tf_op jit(solution)/shard_map/all_gather | solution.py:387
  779.3 95.4 %all-gather.22.cloned.1.call-done = bf16[16,256,1536]{2,1,0:T(8,128)(2,1)} async-done(((bf16[1,256,1536]{2,1,0:T(8,128)(2,1)}), bf16[16,256,1536]{2,1,0:T(8,128)(2,1)}) %all-gather.22.cloned.1.call-update) | async-done | bytes 12582928 | tf_op jit(solution)/shard_map/all_gather | solution.py:117
  994.1 24.5 %copy.220 = bf16[256,12,512]{1,2,0:T(8,128)(2,1)} copy(bf16[256,12,512]{2,1,0:T(8,128)(2,1)} %reshape.745) | data formatting | bytes 6291456 | tf_op jit(solution)/shard_map/reshape | solution.py:89
  1018.6 24.3 copy.201
  1063.6 35.4 %reduce-scatter.27.cloned.1.call-done = bf16[1,256,1536]{1,2,0:T(8,128)(2,1)} async-done(((bf16[16,256,1536]{1,2,0:T(8,128)(2,1)}), bf16[1,256,1536]{1,2,0:T(8,128)(2,1)}) %reduce-scatter.27.cloned.1.call-update) | async-done | bytes 786448 | tf_op jit(solution)/shard_map/reduce_scatter | solution.py:242
  1101.3 135.4 %reduce-scatter.19.cloned.1.call-done = bf16[1,256,1536]{1,2,0:T(8,128)(2,1)} async-done(((bf16[16,256,1536]{1,2,0:T(8,128)(2,1)}), bf16[1,256,1536]{1,2,0:T(8,128)(2,1)}) %reduce-scatter.19.cloned.1.call-update) | async-done | bytes 786448 | tf_op jit(solution)/shard_map/reduce_scatter | solution.py:242
  1255.9 32.0 %copy.221 = f32[256,12,512]{1,2,0:T(8,128)} copy(f32[256,12,512]{0,2,1:T(8,128)} %convolution_bitcast_fusion.4) | data formatting | bytes 12582912 | tf_op jit(solution)/shard_map/rihe,rjhe->ihj/transpose | solution.py:269
  1294.8 37.5 %copy.223 = f32[256,12,512]{2,1,0:T(8,128)} copy(f32[256,12,512]{1,2,0:T(8,128)} %scatter_fusion.1) | data formatting | bytes 12582912 | tf_op jit(solution)/shard_map/scatter-add | solution.py:272
  1350.4 32.2 %copy.202 = f32[256,12,512]{1,2,0:T(8,128)} copy(f32[256,12,512]{0,2,1:T(8,128)} %convolution_bitcast_fusion.5) | data formatting | bytes 12582912 | tf_op jit(solution)/shard_map/rihe,rjhe->ihj/transpose | solution.py:269
  1389.5 37.7 %copy.204 = f32[256,12,512]{2,1,0:T(8,128)} copy(f32[256,12,512]{1,2,0:T(8,128)} %scatter_fusion) | data formatting | bytes 12582912 | tf_op jit(solution)/shard_map/scatter-add | solution.py:272
  1439.9 80.6 %reduce-scatter.21.cloned.1.call-done = f32[192,512]{1,0:T(8,128)} async-done(((f32[3072,512]{1,0:T(8,128)}), f32[192,512]{1,0:T(8,128)}) %reduce-scatter.21.cloned.1.call-update) | async-done | bytes 393232 | tf_op jit(solution)/shard_map/reduce_scatter | solution.py:278
  1529.3 38.3 %all-gather.36.cloned.1.call-done = bf16[3072,512]{1,0:T(8,128)(2,1)} async-done(((bf16[192,512]{1,0:T(8,128)(2,1)}), bf16[3072,512]{1,0:T(8,128)(2,1)}) %all-gather.36.cloned.1.call-update) | async-done | bytes 3145744 | tf_op jit(solution)/shard_map/all_gather | solution.py:282
  1587.5 26.8 %all-gather.28.cloned.1.call-done = bf16[3072,512]{1,0:T(8,128)(2,1)} async-done(((bf16[192,512]{1,0:T(8,128)(2,1)}), bf16[3072,512]{1,0:T(8,128)(2,1)}) %all-gather.28.cloned.1.call-update) | async-done | bytes 3145744 | tf_op jit(solution)/shard_map/all_gather | solution.py:282
  1677.4 26.9 %reduce-scatter.23.cloned.1.call-done = f32[1,256,1536]{1,2,0:T(8,128)} async-done(((f32[1,512,1536]{1,2,0:T(8,128)}), f32[1,256,1536]{1,2,0:T(8,128)}) %reduce-scatter.23.cloned.1.call-update) | async-done | bytes 1572880 | tf_op jit(solution)/shard_map/reduce_scatter | solution.py:294
  1748.0 97.9 %reduce-scatter.39.cloned.1.call-done = f32[3072,24]{0,1:T(8,128)} async-done(((f32[3072,768]{0,1:T(8,128)}), f32[3072,24]{0,1:T(8,128)}) %reduce-scatter.39.cloned.1.call-update) | async-done | bytes 294928 | tf_op jit(solution)/shard_map/reduce_scatter | solution.py:425
  1847.5 139.9 %reduce-scatter.37.cloned.1.call-done = f32[24,3072]{1,0:T(8,128)} async-done(((f32[768,3072]{1,0:T(8,128)}), f32[24,3072]{1,0:T(8,128)}) %reduce-scatter.37.cloned.1.call-update) | async-done | bytes 294928 | tf_op jit(solution)/shard_map/reduce_scatter | solution.py:424
  1989.2 109.7 %reduce-scatter.35.cloned.1.call-done = f32[2,24,768]{2,1,0:T(8,128)} async-done(((f32[2,768,768]{2,1,0:T(8,128)}), f32[2,24,768]{2,1,0:T(8,128)}) %reduce-scatter.35.cloned.1.call-update) | async-done | bytes 147472 | tf_op jit(solution)/shard_map/reduce_scatter | solution.py:423
  2100.7 40.3 %all-reduce.1 = f32[8,768]{1,0:T(8,128)S(1)} all-reduce(f32[8,768]{1,0:T(8,128)S(1)} %add.506), channel_id=15, replica_groups=mesh['seq'=16,'col'=2] {'seq','col'}, use_global_device_ids=true, to_apply=%region_86.88.clone | all-reduce | flops 6144 | bytes 49152
  2141.6 57.4 %reduce-scatter.41.cloned.1.call-done = f32[33,24]{0,1:T(8,128)} async-done(((f32[33,768]{0,1:T(8,128)}), f32[33,24]{0,1:T(8,128)}) %reduce-scatter.41.cloned.1.call-update) | async-done | bytes 3184
  2200.4 166.7 %reduce-scatter.33.cloned.1.call-done = f32[2,24,2304]{2,1,0:T(8,128)} async-done(((f32[2,768,2304]{2,1,0:T(8,128)}), f32[2,24,2304]{2,1,0:T(8,128)}) %reduce-scatter.33.cloned.1.call-update) | async-done | bytes 442384 | tf_op jit(solution)/shard_map/reduce_scatter | solution.py:422
  2372.7 40.8 %all-reduce.2 = (f32[]{:T(128)}, f32[13]{0:T(128)S(1)}, f32[1]{0:T(128)}, f32[1]{0:T(128)}) all-reduce(f32[]{:T(128)S(6)} %add.507, f32[13]{0:T(128)} %maximum_add_fusion.2, f32[1]{0:T(128)} %bitcast.126, f32[1]{0:T(128)} %bitcast.124), channel_id=1, replica_groups=mesh['seq'=16,'col'=2] {'seq','col'}, use_global_device_ids=true, to_apply=%region_88.90 | all-reduce | flops 16 | bytes 128 | tf_op jit(solution)/shard_map/psum | solution.py:433
  (766 shorter events, 528.4 us)
Async XLA Ops:
  7.2 141.1 %all-gather.14.cloned.1.call-start = ((), (), s32[]{:S(2)}) async-start(), calls=%async_computation.13 | async-start | bytes 7299072 | tf_op jit(solution)/shard_map/all_gather | solution.py:384
  9.0 169.0 %all-gather.30.cloned.1.call-start = ((), (), s32[]{:S(2)}) async-start(), calls=%async_computation.25 | async-start | bytes 2359296 | tf_op jit(solution)/shard_map/all_gather | solution.py:75
  146.1 768.8 %copy-start.111 = (f32[768]{0:T(1024)}, f32[768]{0:T(1024)S(1)}, u32[]{:S(2)}) copy-start(f32[768]{0:T(1024)S(1)} %get-tuple-element.55) | copy-start | bytes 9220
  146.1 794.7 %copy-start.103 = (f32[768]{0:T(1024)}, f32[768]{0:T(1024)S(1)}, u32[]{:S(2)}) copy-start(f32[768]{0:T(1024)S(1)} %get-tuple-element.56) | copy-start | bytes 9220
  152.6 54.2 %all-gather.16.cloned.1.call-start = ((), (), s32[]{:S(2)}) async-start(), calls=%async_computation.14 | async-start | bytes 2359296 | tf_op jit(solution)/shard_map/all_gather | solution.py:75
  157.8 138.0 %reduce-scatter.25.cloned.1.call-start = ((), (), s32[]{:S(2)}) async-start(), calls=%async_computation.26 | async-start | bytes 6684672 | tf_op jit(solution)/shard_map/reduce_scatter | solution.py:85
  198.6 186.2 %reduce-scatter.17.cloned.1.call-start = ((), (), s32[]{:S(2)}) async-start(), calls=%async_computation.15 | async-start | bytes 6684672 | tf_op jit(solution)/shard_map/reduce_scatter | solution.py:85
  227.9 203.9 %all-gather.32.cloned.1.call-start = ((), (), s32[]{:S(2)}) async-start(), calls=%async_computation.27 | async-start | bytes 3342336 | tf_op jit(solution)/shard_map/all_gather | solution.py:89
  300.0 191.5 %all-gather.20.cloned.1.call-start = ((), (), s32[]{:S(2)}) async-start(), calls=%async_computation.17 | async-start | bytes 2433024 | tf_op jit(solution)/shard_map/all_gather | solution.py:385
  300.8 237.7 %all-gather.18.cloned.1.call-start = ((), (), s32[]{:S(2)}) async-start(), calls=%async_computation.16 | async-start | bytes 3342336 | tf_op jit(solution)/shard_map/all_gather | solution.py:89
  389.0 252.8 %all-gather.34.cloned.1.call-start = ((), (), s32[]{:S(2)}) async-start(), calls=%async_computation.28 | async-start | bytes 13369344 | tf_op jit(solution)/shard_map/all_gather | solution.py:117
  499.5 207.5 %all-gather.24.cloned.1.call-start = ((), (), s32[]{:S(2)}) async-start(), calls=%async_computation.19 | async-start | bytes 4866048 | tf_op jit(solution)/shard_map/all_gather | solution.py:386
  501.2 271.7 %all-gather.26.cloned.1.call-start = ((), (), s32[]{:S(2)}) async-start(), calls=%async_computation.20 | async-start | bytes 4866048 | tf_op jit(solution)/shard_map/all_gather | solution.py:387
  502.0 372.7 %all-gather.22.cloned.1.call-start = ((), (), s32[]{:S(2)}) async-start(), calls=%async_computation.18 | async-start | bytes 13369344 | tf_op jit(solution)/shard_map/all_gather | solution.py:117
  555.5 543.5 %reduce-scatter.27.cloned.1.call-start = ((), (), s32[]{:S(2)}) async-start(), calls=%async_computation.29 | async-start | bytes 13369344 | tf_op jit(solution)/shard_map/reduce_scatter | solution.py:242
  966.1 270.6 %reduce-scatter.19.cloned.1.call-start = ((), (), s32[]{:S(2)}) async-start(), calls=%async_computation.21 | async-start | bytes 13369344 | tf_op jit(solution)/shard_map/reduce_scatter | solution.py:242
  992.8 443.1 %reduce-scatter.29.cloned.1.call-start = ((), (), s32[]{:S(2)}) async-start(), calls=%async_computation.30 | async-start | bytes 6684672 | tf_op jit(solution)/shard_map/reduce_scatter | solution.py:278
  1340.8 179.7 %reduce-scatter.21.cloned.1.call-start = ((), (), s32[]{:S(2)}) async-start(), calls=%async_computation.22 | async-start | bytes 6684672 | tf_op jit(solution)/shard_map/reduce_scatter | solution.py:278
  1435.8 131.7 %all-gather.36.cloned.1.call-start = ((), (), s32[]{:S(2)}) async-start(), calls=%async_computation.31 | async-start | bytes 3342336 | tf_op jit(solution)/shard_map/all_gather | solution.py:282
  1439.9 174.4 %all-gather.28.cloned.1.call-start = ((), (), s32[]{:S(2)}) async-start(), calls=%async_computation.23 | async-start | bytes 3342336 | tf_op jit(solution)/shard_map/all_gather | solution.py:282
  1523.6 147.1 %reduce-scatter.31.cloned.1.call-start = ((), (), s32[]{:S(2)}) async-start(), calls=%async_computation.32 | async-start | bytes 4718592 | tf_op jit(solution)/shard_map/reduce_scatter | solution.py:294
  1581.8 122.4 %reduce-scatter.23.cloned.1.call-start = ((), (), s32[]{:S(2)}) async-start(), calls=%async_computation.24 | async-start | bytes 4718592 | tf_op jit(solution)/shard_map/reduce_scatter | solution.py:294
  1629.1 216.8 %reduce-scatter.39.cloned.1.call-start = ((), (), s32[]{:S(2)}) async-start(), calls=%async_computation.36 | async-start | bytes 9732096 | tf_op jit(solution)/shard_map/reduce_scatter | solution.py:425
  1638.7 348.8 %reduce-scatter.37.cloned.1.call-start = ((), (), s32[]{:S(2)}) async-start(), calls=%async_computation.35 | async-start | bytes 9732096 | tf_op jit(solution)/shard_map/reduce_scatter | solution.py:424
  1648.1 450.8 %reduce-scatter.35.cloned.1.call-start = ((), (), s32[]{:S(2)}) async-start(), calls=%async_computation.34 | async-start | bytes 4866048 | tf_op jit(solution)/shard_map/reduce_scatter | solution.py:423
  1654.4 544.6 %reduce-scatter.41.cloned.1.call-start = ((), (), s32[]{:S(2)}) async-start(), calls=%async_computation.37 | async-start | bytes 405504
  1724.6 642.5 %reduce-scatter.33.cloned.1.call-start = ((), (), s32[]{:S(2)}) async-start(), calls=%async_computation.33 | async-start | bytes 14598144 | tf_op jit(solution)/shard_map/reduce_scatter | solution.py:422
  1741.5 681.1 %copy-start.95 = (f32[2,24,768]{2,1,0:T(8,128)S(1)}, f32[2,24,768]{2,1,0:T(8,128)}, u32[]{:S(2)}) copy-start(f32[2,24,768]{2,1,0:T(8,128)} %param.35) | copy-start | bytes 442372
  1741.6 683.0 %copy-start.85 = (f32[3072,24]{0,1:T(8,128)S(1)}, f32[3072,24]{0,1:T(8,128)}, u32[]{:S(2)}) copy-start(f32[3072,24]{0,1:T(8,128)} %param.41) | copy-start | bytes 884740
  1741.6 683.0 %copy-start.113 = (f32[3072,24]{0,1:T(8,128)S(1)}, f32[3072,24]{0,1:T(8,128)}, u32[]{:S(2)}) copy-start(f32[3072,24]{0,1:T(8,128)} %param.42) | copy-start | bytes 884740
  1741.6 683.0 %copy-start.114 = (f32[3072,24]{0,1:T(8,128)S(1)}, f32[3072,24]{0,1:T(8,128)}, u32[]{:S(2)}) copy-start(f32[3072,24]{0,1:T(8,128)} %param.43) | copy-start | bytes 884740
  1741.6 685.0 %copy-start.86 = (f32[24,3072]{1,0:T(8,128)S(1)}, f32[24,3072]{1,0:T(8,128)}, u32[]{:S(2)}) copy-start(f32[24,3072]{1,0:T(8,128)} %param.38) | copy-start | bytes 884740
  (218 other events, 11854.6 us)
Sparse Core Ops, SparseCore 0:
  11.5 76.5 all-gather.13
  152.7 25.2 all-gather.29
  179.5 27.1 all-gather.15
  210.6 85.2 reduce-scatter.24
  300.2 84.5 reduce-scatter.16
  387.5 44.3 all-gather.31
  435.3 56.1 all-gather.19
  494.4 44.0 all-gather.17
  540.8 100.9 all-gather.33
  645.1 61.7 all-gather.23
  710.4 62.4 all-gather.25
  775.0 99.5 all-gather.21
  966.2 132.7 reduce-scatter.26
  1102.9 133.7 reduce-scatter.18
  1340.9 84.4 reduce-scatter.28
  1435.9 84.4 reduce-scatter.20
  1523.2 44.3 all-gather.35
  1570.3 43.9 all-gather.27
  1616.5 42.1 reduce-scatter.30
  1660.9 43.3 reduce-scatter.22
  1710.2 135.6 reduce-scatter.38
  1852.8 134.5 reduce-scatter.36
  1992.9 105.9 reduce-scatter.34
  2105.1 93.9 reduce-scatter.40
  2205.1 161.9 reduce-scatter.32
where the time goes:
time: 2450 us; the launch traced here: 2440 us
  waiting for transfers between devices  1440 us (59%)
  local copies, waits for them, and re-layouts  371 us (15%)
  blocking collectives  257 us (10%)
  other arithmetic  170 us (7%)
  matrix products  165 us (7%)
  between operations  28.3 us (1%)
    reduce_scatter x2, waiting for transfers between devices, backward(): lax.psum_scatter(jnp.concatenate([grad_key.reshape(all_rows, cols, D), gr...  171 us
    reduce_scatter x1, waiting for transfers between devices, shards(): lax.psum_scatter(sums[0], ('seq', 'col'), scatter_dimension=1, tiled=True)  167 us
    reduce_scatter x2, waiting for transfers between devices, forward(): lax.psum_scatter(partial_score.reshape(cols * HEADS, C), 'seq', scatter_d...  152 us
    reduce_scatter x1, waiting for transfers between devices, shards(): lax.psum_scatter(sums[2], ('seq', 'col'), scatter_dimension=0, tiled=True)  140 us
    all_gather x2, waiting for transfers between devices, forward(): col_pair = lax.all_gather(col_proj[..., D:], 'seq', axis=0, tiled=True)  135 us
    reduce_scatter x1, waiting for transfers between devices, shards(): lax.psum_scatter(sums[1], ('seq', 'col'), scatter_dimension=1, tiled=True)  110 us
    reduce_scatter x1, waiting for transfers between devices, shards(): lax.psum_scatter(sums[3], ('seq', 'col'), scatter_dimension=1, tiled=True)  97.9 us
    reduce_scatter x2, waiting for transfers between devices, backward(): lax.psum_scatter(partial_grad.reshape(cols * HEADS, C), 'seq', scatter_di...  80.6 us
  transfers between devices with their start and end apart: 25, of which 22 were waited for; matrix products, arithmetic and copies ran while one was open for 20% of the time, Pallas kernels for 0%

commit v1 on v0

v1 whole, which is shorter than its diff:
```python
import jax
import jax.numpy as jnp
from jax import lax
from jax.sharding import PartitionSpec as P

D = 768
HEADS = 12
HD = 64
FF = 3072
VOCAB = 33
VP = 64
STEP = 10

NORM_EPS = 1e-05
MASK_ID = 32
MAX_NORM = 0.001
LEARN_RATE = 0.05
VECTOR_RATE = 0.5
BETA_ONE = 0.9
BETA_TWO = 0.95
ADAM_EPS = 1e-08
WEIGHT_DECAY = 0.01
PRECISE = lax.Precision.HIGHEST
F32 = jnp.float32
BF16 = jnp.bfloat16


def nn(left, right):
    return lax.dot_general(left, right, (((1,), (0,)), ((), ())), preferred_element_type=F32)


def tn(left, right):
    return lax.dot_general(left, right, (((0,), (0,)), ((), ())), preferred_element_type=F32)


def nt(left, right):
    return lax.dot_general(left, right, (((1,), (1,)), ((), ())), preferred_element_type=F32)


def split_two(values):
    high = values.astype(BF16)
    return high, (values - high.astype(F32)).astype(BF16)


def norm_stats(values):
    centre = values - jnp.mean(values, -1, keepdims=True)
    rstd = lax.rsqrt(jnp.mean(centre * centre, -1, keepdims=True) + NORM_EPS)
    return centre * rstd, rstd


def norm_back(unit, rstd, scale_vec, upstream):
    inner = upstream * scale_vec
    grad = rstd * (
        inner - jnp.mean(inner, -1, keepdims=True) - unit * jnp.mean(inner * unit, -1, keepdims=True)
    )
    return grad, jnp.sum(upstream * unit, 0), jnp.sum(upstream, 0)


GELU_K = 0.7978845608028654
GELU_C = 0.044715


def gelu_parts(up):
    square = up * up
    bent = jnp.tanh(GELU_K * up * (1.0 + GELU_C * square))
    half = 0.5 * (1.0 + bent)
    slope = half + 0.5 * up * (1.0 - bent * bent) * GELU_K * (1.0 + 3.0 * GELU_C * square)
    return up * half, slope


def heads_of(block, head):
    return block[:, head * HD : (head + 1) * HD]


def step(big, table, norms, contact_head, ids_all, ids_ri, ids_ir, targets_ir, pair_first, pair_second, labels, counts, cw):
    in_row, in_col, out_row, out_col, up_w, down_t = big
    rows, cols = ids_all.shape
    here = rows * cw
    row_scale = (HD * rows) ** (-0.5)
    vocab = jnp.arange(VP)[:, None]
    hot_all = (ids_all[:, None, :] == vocab[None]).astype(BF16).reshape(rows * VP, cols)
    hot_ri = (ids_ri[None, :] == vocab).astype(BF16)
    hot_ir = (ids_ir[None, :] == vocab).astype(BF16)
    spot = jnp.arange(here)
    perm = (
        ((spot // rows)[:, None] == (spot % cw)[None, :])
        & ((spot % rows)[:, None] == (spot // cw)[None, :])
    ).astype(BF16)

    def to_heads(block):
        return block.reshape(rows, cw, HEADS, VP).transpose(2, 1, 0, 3).reshape(HEADS * cw, rows * VP)

    def to_tokens(block):
        return block.reshape(HEADS, cw, rows, VP).transpose(2, 1, 0, 3).reshape(here, HEADS * VP)

    def per_head(block, other, how):
        return jnp.concatenate(
            [how(heads_of(block, h), heads_of(other, h)) for h in range(HEADS)], -1
        )

    table_f = table.astype(F32)
    unit_t, rstd_t = norm_stats(table_f)
    normed_t = (unit_t * norms[0] + norms[4]).astype(BF16)
    proj_t = nn(normed_t, in_row).astype(BF16)
    query_t, key_t, value_t = proj_t[:, :D], proj_t[:, D : 2 * D], proj_t[:, 2 * D :]

    pair_t = per_head(query_t, key_t, nt)
    pair_hi, pair_lo = split_two(pair_t)
    left_hi = to_heads(tn(hot_ri, pair_hi).astype(BF16))
    left_lo = to_heads(tn(hot_ri, pair_lo).astype(BF16))
    score = (nn(left_hi, hot_all) + nn(left_lo, hot_all)) * row_scale
    prob = jax.nn.softmax(score, axis=-1)
    prob_low = prob.astype(BF16)
    weight_t = to_tokens(nt(prob_low, hot_all))
    weight_hi, weight_lo = split_two(weight_t)
    row_mixed_ri = (
        per_head(weight_hi, value_t, nn) + per_head(weight_lo, value_t, nn)
    ).astype(BF16)
    row_mixed = nn(perm, row_mixed_ri).astype(BF16)
    embedded = tn(hot_ir, table)
    after_row = embedded + nn(row_mixed, out_row)

    prob_cube = prob_low.astype(F32).reshape(HEADS, cw, cols)
    head_sum = jnp.sum(prob_cube * contact_head[:HEADS, None, None], 0)
    first_hot = (pair_first[None, :] == jnp.arange(cw)[:, None]).astype(F32)
    second_hot = (pair_second[None, :] == jnp.arange(cols)[:, None]).astype(BF16)
    sum_hi, sum_lo = split_two(head_sum)
    sum_last = (head_sum - sum_hi.astype(F32) - sum_lo.astype(F32)).astype(BF16)
    picked = nn(sum_hi, second_hot) + nn(sum_lo, second_hot) + nn(sum_last, second_hot)
    contact_logit = jnp.sum(picked * first_hot, 0) * cols + contact_head[HEADS]
    owned = jnp.sum(first_hot, 0) > 0
    valid = (labels >= 0) & owned
    positive = (labels == 1).astype(F32)
    bce_sum = jnp.sum(
        jnp.where(valid, jax.nn.softplus(contact_logit) - positive * contact_logit, 0.0)
    )
    coef = jnp.where(valid, jax.nn.sigmoid(contact_logit) - positive, 0.0) / counts[1]
    coef_hi, coef_lo = split_two(coef)
    first_low = first_hot.astype(BF16)
    touch = nt(first_low * coef_hi[None], second_hot) + nt(first_low * coef_lo[None], second_hot)
    grad_contact = jnp.concatenate(
        [jnp.sum(prob_cube * touch[None], (1, 2)) * cols, jnp.sum(coef)[None]]
    )

    unit_1, rstd_1 = norm_stats(after_row)
    col_normed = (unit_1 * norms[1] + norms[5]).astype(BF16)
    col_proj = nn(col_normed, in_col).astype(BF16)
    group = 128 if here % 128 == 0 and 128 % rows == 0 else here
    groups = here // group
    lane = jnp.arange(group)
    same = (lane[:, None] // rows) == (lane[None, :] // rows)

    def cut(block):
        return block.reshape(groups, group, HEADS, HD)

    col_query, col_key, col_value = (cut(col_proj[:, k * D : (k + 1) * D]) for k in range(3))
    col_score = jnp.einsum("gqhe,gkhe->ghqk", col_query, col_key, preferred_element_type=F32) * HD ** (-0.5)
    col_prob = jax.nn.softmax(jnp.where(same, col_score, -1e30), axis=-1)
    col_prob_low = col_prob.astype(BF16)
    col_mixed = (
        jnp.einsum("ghqk,gkhe->gqhe", col_prob_low, col_value, preferred_element_type=F32)
        .astype(BF16)
        .reshape(here, D)
    )
    after_col = after_row + nn(col_mixed, out_col)

    unit_2, rstd_2 = norm_stats(after_col)
    feed_normed = (unit_2 * norms[2] + norms[6]).astype(BF16)
    hidden_up = nn(feed_normed, up_w)
    active, slope = gelu_parts(hidden_up)
    active = active.astype(BF16)
    after_feed = after_col + nt(active, down_t)
    unit_3, rstd_3 = norm_stats(after_feed)
    head_normed = (unit_3 * norms[3] + norms[7]).astype(BF16)
    logits = nt(table, head_normed) * D ** (-0.5)
    logits = jnp.where(vocab < VOCAB, logits, -1e30)
    top = jnp.max(logits, 0, keepdims=True)
    shifted = logits - top
    log_probs = shifted - jnp.log(jnp.sum(jnp.exp(shifted), 0, keepdims=True))
    target_hot = (targets_ir[None, :] == vocab).astype(F32)
    keep = ids_ir[None, :] == MASK_ID
    mlm_sum = -jnp.sum(jnp.where(keep & (target_hot > 0), log_probs, 0.0))
    logit_grad = jnp.where(keep, jnp.exp(log_probs) - target_hot, 0.0) / counts[0]
    logit_low = (logit_grad * D ** (-0.5)).astype(BF16)

    grad_head = nn(logit_low, head_normed)
    stream, scale_3, shift_3 = norm_back(unit_3, rstd_3, norms[3], tn(logit_low, table))
    branch = stream.astype(BF16)
    grad_down = tn(branch, active)
    up_low = (nn(branch, down_t) * slope).astype(BF16)
    grad_up = tn(feed_normed, up_low)
    inner, scale_2, shift_2 = norm_back(unit_2, rstd_2, norms[2], nt(up_low, up_w))
    stream = stream + inner
    branch = stream.astype(BF16)
    grad_out_col = tn(col_mixed, branch)
    mixed_low = nt(branch, out_col).astype(BF16)
    mixed_cut = cut(mixed_low)
    prob_grad = jnp.einsum("gqhe,gkhe->ghqk", mixed_cut, col_value, preferred_element_type=F32)
    score_grad = col_prob * (prob_grad - jnp.sum(col_prob * prob_grad, -1, keepdims=True))
    score_low = score_grad.astype(BF16)
    grad_q = jnp.einsum("ghqk,gkhe->gqhe", score_low, col_key, preferred_element_type=F32)
    grad_k = jnp.einsum("ghqk,gqhe->gkhe", score_low, col_query, preferred_element_type=F32)
    grad_v = jnp.einsum("ghqk,gqhe->gkhe", col_prob_low, mixed_cut, preferred_element_type=F32)
    proj_low = jnp.concatenate(
        [
            (grad_q * HD ** (-0.5)).reshape(here, D),
            (grad_k * HD ** (-0.5)).reshape(here, D),
            grad_v.reshape(here, D),
        ],
        -1,
    ).astype(BF16)
    grad_in_col = tn(col_normed, proj_low)
    inner, scale_1, shift_1 = norm_back(unit_1, rstd_1, norms[1], nt(proj_low, in_col))
    stream = stream + inner
    branch = stream.astype(BF16)
    grad_out_row = tn(row_mixed, branch)
    mixed_low = nt(branch, out_row).astype(BF16)
    mixed_ri = tn(perm, mixed_low).astype(BF16)
    drive_hi, drive_lo = split_two(per_head(mixed_ri, value_t, nt))
    prob_grad = nn(to_heads(drive_hi), hot_all) + nn(to_heads(drive_lo), hot_all)
    prob_grad = prob_grad + (
        touch[None] * (contact_head[:HEADS, None, None] * cols)
    ).reshape(HEADS * cw, cols)
    score_grad = prob * (prob_grad - jnp.sum(prob * prob_grad, -1, keepdims=True))
    score_low = score_grad.astype(BF16)
    spread = to_tokens(nt(score_low, hot_all)).astype(BF16)
    table_pair = nn(hot_ri, spread)
    value_grad = per_head(weight_hi, mixed_ri, tn)
    stream_hi, stream_lo = split_two(stream)
    lookup_grad = nn(hot_ir, stream_hi) + nn(hot_ir, stream_lo)
    vectors = jnp.stack([scale_1, scale_2, scale_3, shift_1, shift_2, shift_3])
    return (
        (grad_in_col, grad_out_row, grad_out_col, grad_up, grad_down),
        (table_pair, value_grad, grad_head + lookup_grad, vectors),
        grad_contact,
        mlm_sum,
        bce_sum,
        (unit_t, rstd_t, normed_t, query_t, key_t),
    )


def adam_update(master, first, second, grad_part, rate):
    first = BETA_ONE * first + (1.0 - BETA_ONE) * grad_part
    second = BETA_TWO * second + (1.0 - BETA_TWO) * grad_part * grad_part
    moved = first / (1.0 - BETA_ONE**STEP) / (jnp.sqrt(second / (1.0 - BETA_TWO**STEP)) + ADAM_EPS)
    return (master - rate * (moved + WEIGHT_DECAY * master), first, second)


def shards(
    tokens,
    targets,
    masked,
    contact_pairs,
    labels,
    attention_in_master,
    attention_in_first,
    attention_in_second,
    attention_out_master,
    attention_out_first,
    attention_out_second,
    feed_up_master,
    feed_up_first,
    feed_up_second,
    feed_down_master,
    feed_down_first,
    feed_down_second,
    embedding_master,
    embedding_first,
    embedding_second,
    norm_params_master,
    norm_params_first,
    norm_params_second,
    contact_head_master,
    contact_head_first,
    contact_head_second,
):
    both = ("seq", "col")
    micro, rows_here, cols_here = tokens.shape
    ncol = lax.axis_size("col")
    ndev = lax.axis_size("seq") * ncol
    cols = cols_here * ncol
    me = lax.axis_index("seq") * ncol + lax.axis_index("col")
    per = ndev // micro
    cw = cols // per
    mine = me // per
    base = (me % per) * cw
    shard = D // ndev

    inputs = jnp.where(masked > 0, MASK_ID, tokens)
    whole = jnp.stack([inputs, targets])
    whole = lax.all_gather(lax.all_gather(whole, "col", axis=3, tiled=True), "seq", axis=2, tiled=True)
    pairs_all = lax.all_gather(
        jnp.concatenate([contact_pairs, labels[:, :, None]], -1), both, axis=1, tiled=True
    )
    counts = (
        jnp.sum(whole[0] == MASK_ID).astype(F32),
        jnp.sum(pairs_all[..., 2] >= 0).astype(F32),
    )
    ids_all = lax.dynamic_index_in_dim(whole[0], mine, 0, False)
    ids_local = lax.dynamic_slice_in_dim(ids_all, base, cw, 1)
    targets_local = lax.dynamic_slice_in_dim(
        lax.dynamic_index_in_dim(whole[1], mine, 0, False), base, cw, 1
    )
    pairs = lax.dynamic_index_in_dim(pairs_all, mine, 0, False)

    flat = jnp.concatenate(
        [
            attention_in_master[0],
            attention_in_master[1],
            attention_out_master[0],
            attention_out_master[1],
            feed_up_master,
            feed_down_master.T,
            jnp.pad(embedding_master.T, ((0, 0), (0, VP - VOCAB))),
            jnp.pad(norm_params_master.T, ((0, 0), (0, VP - 8))),
        ],
        1,
    ).astype(BF16)
    full = lax.all_gather(flat, both, axis=0, tiled=True)
    edges = [0, 3 * D, 6 * D, 7 * D, 8 * D, 8 * D + FF, 8 * D + 2 * FF]
    big = [full[:, a:b] for a, b in zip(edges[:-1], edges[1:])]
    in_row = big[0]
    table = full[:, edges[-1] : edges[-1] + VP].T
    norms = full[:, edges[-1] + VP : edges[-1] + VP + 8].T.astype(F32)

    grads, tables, contact_total, mlm_total, bce_total, kept = step(
        big,
        table,
        norms,
        contact_head_master,
        ids_all,
        ids_local.reshape(-1),
        ids_local.T.reshape(-1),
        targets_local.T.reshape(-1),
        pairs[:, 0] - base,
        pairs[:, 1],
        pairs[:, 2],
        counts,
        cw,
    )
    flat_grad = jnp.concatenate([g.astype(BF16) for g in grads], 1)
    reduced = lax.psum_scatter(flat_grad, both, scatter_dimension=0, tiled=True).astype(F32)
    table_pair, value_grad, table_grad, vectors, contact_grad, mlm_total, bce_total = lax.psum(
        (*tables, contact_total, mlm_total, bce_total), both
    )
    unit_t, rstd_t, normed_t, query_t, key_t = kept
    row_scale = (HD * ids_all.shape[0]) ** (-0.5)
    query_grad = []
    key_grad = []
    for h in range(HEADS):
        pair = heads_of(table_pair, h)
        query_grad.append(jnp.dot(pair, heads_of(key_t, h).astype(F32), precision=PRECISE))
        key_grad.append(jnp.dot(pair.T, heads_of(query_t, h).astype(F32), precision=PRECISE))
    proj_grad = jnp.concatenate(
        [
            jnp.concatenate(query_grad, 1) * row_scale,
            jnp.concatenate(key_grad, 1) * row_scale,
            value_grad,
        ],
        1,
    )
    proj_hi, proj_lo = split_two(proj_grad)
    normed_grad = nt(proj_hi, in_row) + nt(proj_lo, in_row)
    back_t, scale_0, shift_0 = norm_back(unit_t, rstd_t, norms[0], normed_grad)
    table_grad = table_grad + back_t
    low = me * shard
    normed_mine = lax.dynamic_slice_in_dim(normed_t, low, shard, 1)
    grad_in_row = tn(normed_mine, proj_hi) + tn(normed_mine, proj_lo)
    norm_grad = jnp.concatenate([scale_0[None], vectors[:3], shift_0[None], vectors[3:]])
    table_mine = lax.dynamic_slice_in_dim(table_grad[:VOCAB], low, shard, 1)
    norm_mine = lax.dynamic_slice_in_dim(norm_grad, low, shard, 1)
    cuts = [3 * D, 4 * D, 5 * D, 5 * D + FF]
    g_in_col, g_out_row, g_out_col, g_up, g_down = jnp.split(reduced, cuts, 1)

    local_square = (
        jnp.sum(reduced * reduced)
        + jnp.sum(grad_in_row * grad_in_row)
        + jnp.sum(table_mine * table_mine)
        + jnp.sum(norm_mine * norm_mine)
    )
    square = lax.psum(local_square, both) + jnp.sum(contact_grad * contact_grad)
    grad_norm = jnp.sqrt(square)
    factor = jnp.minimum(1.0, MAX_NORM / grad_norm)
    in_new, in_moment, in_square = adam_update(
        attention_in_master, attention_in_first, attention_in_second, jnp.stack([grad_in_row, g_in_col]) * factor, LEARN_RATE
    )
    out_new, out_moment, out_square = adam_update(
        attention_out_master, attention_out_first, attention_out_second, jnp.stack([g_out_row, g_out_col]) * factor, LEARN_RATE
    )
    up_new, up_moment, up_square = adam_update(
        feed_up_master, feed_up_first, feed_up_second, g_up * factor, LEARN_RATE
    )
    down_new, down_moment, down_square = adam_update(
        feed_down_master, feed_down_first, feed_down_second, g_down.T * factor, LEARN_RATE
    )
    table_new, table_moment, table_square = adam_update(
        embedding_master, embedding_first, embedding_second, table_mine * factor, VECTOR_RATE
    )
    norm_new, norm_moment, norm_square = adam_update(
        norm_params_master, norm_params_first, norm_params_second, norm_mine * factor, VECTOR_RATE
    )
    head_new, head_moment, head_square = adam_update(
        contact_head_master, contact_head_first, contact_head_second, contact_grad * factor, VECTOR_RATE
    )
    loss_parts = jnp.stack([mlm_total, counts[0], bce_total, counts[1]])
    return (
        in_new, in_moment, in_square,
        out_new, out_moment, out_square,
        up_new, up_moment, up_square,
        down_new, down_moment, down_square,
        table_new, table_moment, table_square,
        norm_new, norm_moment, norm_square,
        head_new, head_moment, head_square,
        in_new.astype(BF16), out_new.astype(BF16), up_new.astype(BF16), down_new.astype(BF16), table_new.astype(BF16),
        loss_parts, grad_norm,
    )


def solution(mesh):
    both = ("seq", "col")
    cells = P(None, "seq", "col")
    stack = P(None, both, None)
    row_split = P(both, None)
    col_split = P(None, both)
    weights = [stack] * 6 + [row_split] * 3 + [col_split] * 9 + [P()] * 3
    return jax.shard_map(
        shards,
        mesh=mesh,
        in_specs=(cells, cells, cells, stack, col_split, *weights),
        out_specs=(*weights, stack, stack, row_split, col_split, col_split, P(), P()),
        check_vma=False,
    )
```

time: 2450 us -> 772 us (0.32)
  waiting for transfers between devices: 1440 us -> 239 us
  local copies, waits for them, and re-layouts: 371 us -> 76.1 us
  other arithmetic: 170 us -> 47.6 us
  blocking collectives: 257 us -> 213 us
    reduce_scatter x12 -> x1, waiting for transfers between devices: 944 us -> 149 us  [shards(): lax.psum_scatter(flat_grad, both, scatter_dimension=0, tiled=True)]
    all_gather x12 -> x1, waiting for transfers between devices: 441 us -> 12.4 us  [shards(): full = lax.all_gather(flat, both, axis=0, tiled=True)]
    reshape x26 -> x11, local copies, waits for them, and re-layouts: 109 us -> 27.1 us  [the longest x6 14.4 us: to_heads(): block.reshape(rows, cw, HEADS, VP).transpose(2, 1, 0, 3)]
    psum x0 -> x1, waiting for transfers between devices: none -> 77.2 us  [shards(): lax.psum((*tables, contact_total, mlm_total, bce_total), both)]
    scatter-add x2 -> x0, local copies, waits for them, and re-layouts: 75.1 us -> none  [backward(): partial_grad.at[local_query, :, contact_pairs[:, 1]]]
    unnamed x26 -> x3, waiting for transfers between devices: 57.9 us -> 0.05 us
    transpose x2 -> x9, local copies, waits for them, and re-layouts: 64.1 us -> 13.1 us  [the longest x4 7.96 us: to_heads(): block.reshape(rows, cw, HEADS, VP).transpose(2, 1, 0, 3)]
    unnamed x448 -> x302, local copies, waits for them, and re-layouts: 51.9 us -> 7.1 us
  transfers between devices with their start and end apart: 25 -> 3, of which waited for: 22 -> 3; matrix products, arithmetic and copies ran while one was open for 20% -> 6% of each run, Pallas kernels for 0% -> 0%
where the time goes in v1:
time: 772 us; the launch traced here: 761 us
  waiting for transfers between devices  239 us (31%)
  blocking collectives  213 us (28%)
  matrix products  161 us (21%)
  local copies, waits for them, and re-layouts  76.1 us (10%)
  other arithmetic  47.6 us (6%)
  between operations  23.6 us (3%)
    reduce_scatter x1, waiting for transfers between devices, shards(): lax.psum_scatter(flat_grad, both, scatter_dimension=0, tiled=True)  149 us
    all_gather x1, blocking collectives, shards(): lax.all_gather(jnp.concatenate([contact_pairs, labels[:, :, None]], -1),...  104 us
    psum x1, waiting for transfers between devices, shards(): lax.psum((*tables, contact_total, mlm_total, bce_total), both)  77.2 us
    dot_general x24, matrix products, tn(): lax.dot_general(left, right, (((0,), (0,)), ((), ())), preferred_element_...  51.4 us
    dot_general x42, matrix products, nn(): lax.dot_general(left, right, (((1,), (0,)), ((), ())), preferred_element_...  46.5 us
    dot_general x35, matrix products, nt(): lax.dot_general(left, right, (((1,), (1,)), ((), ())), preferred_element_...  41.9 us
    psum x1, blocking collectives, shards(): lax.psum((*tables, contact_total, mlm_total, bce_total), both)  40.6 us
    psum x1, blocking collectives, shards(): square = lax.psum(local_square, both) + jnp.sum(contact_grad * contact_grad)  40.4 us
  transfers between devices with their start and end apart: 3, of which 3 were waited for; matrix products, arithmetic and copies ran while one was open for 6% of the time, Pallas kernels for 0%

profile of v1, /device:TPU:0, one launch (start us, length us, event | category | flops | bytes accessed | tf_op | source)
XLA Modules:
  0.0 760.6 jit_solution(12738168655520264166)
XLA Ops:
  15.3 5.2 all_gather.13
  20.5 23.0 %all_gather.14 = s32[2,2,16,512]{3,1,0,2:T(2,128)S(1)} all-gather(s32[2,2,1,512]{3,1,0,2:T(2,128)S(1)} %all_gather.13), channel_id=1, replica_groups=mesh['seq'=16,'col'=2] {'seq'}, dimensions={2}, use_global_device_ids=true | all-gather | bytes 139264 | tf_op jit(solution)/shard_map/all_gather | solution.py:291
  46.3 103.8 %all_gather.15 = s32[2,2048,3]{2,0,1:T(2,128)S(1)} all-gather(s32[2,64,3]{2,0,1:T(2,128)S(1)} %pad_add_fusion), channel_id=1, replica_groups=mesh['seq'=16,'col'=2] {'seq','col'}, dimensions={1}, use_global_device_ids=true | all-gather | bytes 50688 | tf_op jit(solution)/shard_map/all_gather | solution.py:292
  150.0 2.9 fusion.28
  159.4 12.4 %all-gather.2.cloned.1.call-done = bf16[768,12416]{1,0:T(8,128)(2,1)} async-done(((bf16[24,12416]{1,0:T(8,128)(2,1)}), bf16[768,12416]{1,0:T(8,128)(2,1)}) %all-gather.2.cloned.1.call-update) | async-done | bytes 19070992 | tf_op jit(solution)/shard_map/all_gather | solution.py:319
  178.2 2.8 convolution_convert_fusion.4
  189.9 3.5 reshape.548
  196.8 3.0 reshape.550
  206.1 4.3 copy.415
  210.3 3.8 reshape.551
  225.5 4.1 convolution_convert_fusion.3
  245.6 3.2 fusion.423
  249.6 7.2 fusion.14
  256.8 6.6 fusion.424
  268.0 7.7 %multiply_convert_fusion = bf16[512,3072]{1,0:T(8,128)(2,1)S(1)} fusion(f32[512,3072]{1,0:T(8,128)} %fusion.14, bf16[768,12416]{1,0:T(8,128)(2,1)S(1)} %bitcast.197, f32[512,768]{1,0:T(8,128)S(1)} %subtract_multiply_fusion), kind=kOutput, calls=%fused_computation.1 | convolution fusion | flops 2444623872 | bytes 15728640 | tf_op jit(solution)/shard_map/dot_general | solution.py:29
  275.7 3.5 multiply_reduce_fusion.2
  285.0 2.9 reshape.556
  287.9 3.4 fusion.58
  297.8 6.0 multiply_reduce_fusion.3
  307.6 4.3 convolution_convert_fusion.13
  329.4 5.8 fusion.3
  354.1 5.5 fusion.29
  374.9 3.2 convert_element_type.341
  379.0 3.2 fusion.50
  384.5 4.8 fusion.2
  392.0 8.0 %fusion.1 = bf16[768,9984]{1,0:T(8,128)(2,1)} fusion(bf16[768,9984]{1,0:T(8,128)(2,1)} %fusion.2, f32[512,768]{1,0:T(8,128)S(1)} %copy-done.16, f32[512,3072]{1,0:T(8,128)} %fusion.14), kind=kOutput, calls=%fused_computation.6 | convolution fusion | flops 2432827392 | bytes 12582912 | tf_op jit(solution)/shard_map/dot_general | solution.py:33
  402.4 40.6 %psum.59 = f32[6,768]{1,0:T(8,128)S(1)} all-reduce(f32[6,768]{1,0:T(8,128)S(1)} %stack.75), channel_id=1, replica_groups=mesh['seq'=16,'col'=2] {'seq','col'}, use_global_device_ids=true, to_apply=%region_43.44 | all-reduce | flops 4608 | bytes 36864 | tf_op jit(solution)/shard_map/psum | solution.py:343
  444.7 77.2 %all-reduce.6.cloned.1.call-done = (f32[64,768]{1,0:T(8,128)}, f32[64,768]{1,0:T(8,128)}, f32[64,768]{0,1:T(8,128)}) async-done(((f32[64,768]{1,0:T(8,128)}, f32[64,768]{1,0:T(8,128)}, f32[64,768]{0,1:T(8,128)}), (f32[64,768]{1,0:T(8,128)}, f32[64,768]{1,0:T(8,128)}, f32[64,768]{0,1:T(8,128)})) %all-reduce.6.cloned.1.call-update) | async-done | bytes 589840 | tf_op jit(solution)/shard_map/psum | solution.py:343
  536.8 3.3 fusion.19
  540.2 3.5 multiply_reduce_fusion.16
  548.1 149.0 %reduce-scatter.2.cloned.1.call-done = bf16[24,9984]{1,0:T(8,128)(2,1)} async-done(((bf16[768,9984]{1,0:T(8,128)(2,1)}), bf16[24,9984]{1,0:T(8,128)(2,1)}) %reduce-scatter.2.cloned.1.call-update) | async-done | bytes 479248 | tf_op jit(solution)/shard_map/reduce_scatter | solution.py:342
  701.8 40.4 %all-reduce.2 = (f32[]{:T(128)}, f32[13]{0:T(128)S(1)}, f32[1]{0:T(128)}, f32[1]{0:T(128)}) all-reduce(f32[]{:T(128)S(6)} %add.427, f32[13]{0:T(128)S(1)} %pad_maximum_fusion.1, f32[1]{0:T(128)} %bitcast.49, f32[1]{0:T(128)} %bitcast.47), channel_id=1, replica_groups=mesh['seq'=16,'col'=2] {'seq','col'}, use_global_device_ids=true, to_apply=%region_46.47 | all-reduce | flops 16 | bytes 128 | tf_op jit(solution)/shard_map/psum | solution.py:381
  (568 shorter events, 178.9 us)
Async XLA Ops:
  7.2 164.6 %all-gather.2.cloned.1.call-start = ((), (), s32[]{:S(2)}) async-start(), calls=%async_computation.1 | async-start | bytes 19666944 | tf_op jit(solution)/shard_map/all_gather | solution.py:319
  13.1 508.9 %all-reduce.6.cloned.1.call-start = ((), (), s32[]{:S(2)}) async-start(), calls=%async_computation.3 | async-start | bytes 1572864 | tf_op jit(solution)/shard_map/psum | solution.py:343
  45.9 137.8 %copy-start.54 = (s32[512]{0:T(512)}, s32[512]{0:T(512)S(1)}, u32[]{:S(2)}) copy-start(s32[512]{0:T(512)S(1)} %eq.225) | copy-start | bytes 6148
  155.7 64.5 %copy-start.95 = (s32[512]{0:T(512)}, s32[512]{0:T(512)S(1)}, u32[]{:S(2)}) copy-start(s32[512]{0:T(512)S(1)} %get-tuple-element.372) | copy-start | bytes 6148
  155.7 64.5 %copy-start.96 = (s32[512]{0:T(512)}, s32[512]{0:T(512)S(1)}, u32[]{:S(2)}) copy-start(s32[512]{0:T(512)S(1)} %get-tuple-element.373) | copy-start | bytes 6148
  155.7 64.5 %copy-start.97 = (s32[512]{0:T(512)}, s32[512]{0:T(512)S(1)}, u32[]{:S(2)}) copy-start(s32[512]{0:T(512)S(1)} %get-tuple-element.370) | copy-start | bytes 6148
  155.7 64.5 %copy-start.98 = (s32[512]{0:T(512)}, s32[512]{0:T(512)S(1)}, u32[]{:S(2)}) copy-start(s32[512]{0:T(512)S(1)} %get-tuple-element.371) | copy-start | bytes 6148
  155.8 21.2 %copy-start.69 = (s32[2048,1]{0,1:T(1,128)}, s32[2048,1]{0,1:T(1,128)S(1)}, u32[]{:S(2)}) copy-start(s32[2048,1]{0,1:T(1,128)S(1)} %get-tuple-element.343) | copy-start | bytes 24580
  155.8 47.7 %copy-start.104 = (s32[2048,1]{0,1:T(1,128)}, s32[2048,1]{0,1:T(1,128)S(1)}, u32[]{:S(2)}) copy-start(s32[2048,1]{0,1:T(1,128)S(1)} %get-tuple-element.344) | copy-start | bytes 24580
  243.6 13.1 %slice-start = ((s8[19070976]{0:T(1024)(128)(4,1)}), s8[4194304]{0:T(1024)(128)(4,1)S(1)}, s32[]{:S(2)}) async-start(s8[19070976]{0:T(1024)(128)(4,1)} %bitcast.196), calls=%async_computation.4 | async-start | bytes 8388608
  243.6 13.1 %slice-start.1 = ((s8[19070976]{0:T(1024)(128)(4,1)}), s8[4194304]{0:T(1024)(128)(4,1)S(1)}, s32[]{:S(2)}) async-start(s8[19070976]{0:T(1024)(128)(4,1)} %bitcast.196), calls=%async_computation.5 | async-start | bytes 8388608
  248.9 30.3 %copy-start.74 = (f32[512]{0:T(512)}, f32[512]{0:T(512)S(1)}, u32[]{:S(2)}) copy-start(f32[512]{0:T(512)S(1)} %broadcast_multiply_fusion.10) | copy-start | bytes 6148
  249.2 30.0 %copy-start.101 = (f32[512]{0:T(512)}, f32[512]{0:T(512)S(1)}, u32[]{:S(2)}) copy-start(f32[512]{0:T(512)S(1)} %add_rsqrt_fusion.1) | copy-start | bytes 6148
  268.0 11.2 %copy-start.15 = (f32[512,768]{1,0:T(8,128)}, f32[512,768]{1,0:T(8,128)S(1)}, u32[]{:S(2)}) copy-start(f32[512,768]{1,0:T(8,128)S(1)} %subtract_multiply_fusion) | copy-start | bytes 4718596
  312.0 11.2 %copy-start.18 = (bf16[512,768]{1,0:T(8,128)(2,1)S(1)}, bf16[512,768]{1,0:T(8,128)(2,1)}, u32[]{:S(2)}) copy-start(bf16[512,768]{1,0:T(8,128)(2,1)} %convolution_convert_fusion.13) | copy-start | bytes 2359300
  317.5 11.7 %copy-start.79 = (f32[512]{0:T(512)S(1)}, f32[512]{0:T(512)}, u32[]{:S(2)}) copy-start(f32[512]{0:T(512)} %copy-done.77) | copy-start | bytes 6148
  317.5 11.7 %copy-start.84 = (f32[768]{0:T(1024)S(1)}, f32[768]{0:T(1024)}, u32[]{:S(2)}) copy-start(f32[768]{0:T(1024)} %get-tuple-element.273) | copy-start | bytes 9220
  317.5 11.7 %copy-start.109 = (f32[512]{0:T(512)S(1)}, f32[512]{0:T(512)}, u32[]{:S(2)}) copy-start(f32[512]{0:T(512)} %copy-done.107) | copy-start | bytes 6148
  317.5 11.7 %copy-start.117 = (f32[768]{0:T(1024)S(1)}, f32[768]{0:T(1024)}, u32[]{:S(2)}) copy-start(f32[768]{0:T(1024)} %get-tuple-element.272) | copy-start | bytes 9220
  391.7 305.4 %reduce-scatter.2.cloned.1.call-start = ((), (), s32[]{:S(2)}) async-start(), calls=%async_computation.2 | async-start | bytes 15814656 | tf_op jit(solution)/shard_map/reduce_scatter | solution.py:342
  400.0 43.7 %copy-start.111 = (f32[64]{0:T(128)S(1)}, f32[64]{0:T(128)}, u32[]{:S(2)}) copy-start(f32[64]{0:T(128)} %copy-done.110) | copy-start | bytes 772
  400.0 43.7 %copy-start.113 = (f32[64]{0:T(128)S(1)}, f32[64]{0:T(128)}, u32[]{:S(2)}) copy-start(f32[64]{0:T(128)} %copy-done.112) | copy-start | bytes 772
  522.0 12.4 %copy-start.19 = (f32[64,768]{1,0:T(8,128)S(1)}, f32[64,768]{1,0:T(8,128)}, u32[]{:S(2)}) copy-start(f32[64,768]{1,0:T(8,128)} %get-tuple-element.283) | copy-start | bytes 589828
  548.0 196.1 %copy-start.135 = (f32[13]{0:T(128)S(1)}, f32[13]{0:T(128)}, u32[]{:S(2)}) copy-start(f32[13]{0:T(128)} %param.49) | copy-start | bytes 160
  548.0 196.1 %copy-start.136 = (f32[13]{0:T(128)S(1)}, f32[13]{0:T(128)}, u32[]{:S(2)}) copy-start(f32[13]{0:T(128)} %param.50) | copy-start | bytes 160
  548.0 196.1 %copy-start.137 = (f32[13]{0:T(128)S(1)}, f32[13]{0:T(128)}, u32[]{:S(2)}) copy-start(f32[13]{0:T(128)} %param.51) | copy-start | bytes 160
  548.0 196.7 %copy-start.26 = (f32[24,3072]{1,0:T(8,128)S(1)}, f32[24,3072]{1,0:T(8,128)}, u32[]{:S(2)}) copy-start(f32[24,3072]{1,0:T(8,128)} %param.37) | copy-start | bytes 884740
  548.0 196.7 %copy-start.44 = (f32[24,3072]{1,0:T(8,128)S(1)}, f32[24,3072]{1,0:T(8,128)}, u32[]{:S(2)}) copy-start(f32[24,3072]{1,0:T(8,128)} %param.38) | copy-start | bytes 884740
  548.0 196.7 %copy-start.45 = (f32[24,3072]{1,0:T(8,128)S(1)}, f32[24,3072]{1,0:T(8,128)}, u32[]{:S(2)}) copy-start(f32[24,3072]{1,0:T(8,128)} %param.39) | copy-start | bytes 884740
  698.2 47.6 %copy-start.27 = (f32[3072,24]{0,1:T(8,128)S(1)}, f32[3072,24]{0,1:T(8,128)}, u32[]{:S(2)}) copy-start(f32[3072,24]{0,1:T(8,128)} %param.40) | copy-start | bytes 884740
  698.3 47.6 %copy-start.46 = (f32[3072,24]{0,1:T(8,128)S(1)}, f32[3072,24]{0,1:T(8,128)}, u32[]{:S(2)}) copy-start(f32[3072,24]{0,1:T(8,128)} %param.41) | copy-start | bytes 884740
  698.3 47.6 %copy-start.47 = (f32[3072,24]{0,1:T(8,128)S(1)}, f32[3072,24]{0,1:T(8,128)}, u32[]{:S(2)}) copy-start(f32[3072,24]{0,1:T(8,128)} %param.42) | copy-start | bytes 884740
  (120 other events, 351.7 us)
Sparse Core Ops, SparseCore 0:
  13.2 158.5 all-gather.1
  391.8 130.1 all-reduce.5
  529.2 167.7 reduce-scatter.1

commit v2 on v1

--- a/solution.py
+++ b/solution.py
@@ -1,6 +1,10 @@
+import functools
+
 import jax
 import jax.numpy as jnp
 from jax import lax
+from jax.experimental import pallas as pl
+from jax.experimental.pallas import tpu as pltpu
 from jax.sharding import PartitionSpec as P
 
 D = 768
@@ -239,6 +243,393 @@
     )
 
 
+MESH = pl.DeviceIdType.MESH
+NZ, NY = 4, 2
+
+
+def place():
+    s, c = lax.axis_index("seq"), lax.axis_index("col")
+    z, y, k = s // 4, lax.rem(s // 2, 2), lax.rem(s, 2)
+    return z, y, k, c
+
+
+def device(z, y, k, c):
+    return (z * 4 + y * 2 + k, c)
+
+
+def greet_all():
+    z, y, k, c = place()
+    me = (z * 4 + y * 2 + k) * 2 + c
+    barrier = pltpu.get_barrier_semaphore()
+
+    def signal(step, carry):
+        other = lax.rem(me + step, 32)
+        pl.semaphore_signal(
+            barrier, inc=1, device_id=(other // 2, lax.rem(other, 2)), device_id_type=MESH
+        )
+        return carry
+
+    lax.fori_loop(1, 32, signal, 0)
+    return barrier
+
+
+def remote(src, dst, send, recv, target):
+    return pltpu.make_async_remote_copy(
+        src_ref=src, dst_ref=dst, send_sem=send, recv_sem=recv, device_id=target, device_id_type=MESH
+    )
+
+
+def gather_kernel(widths, *refs):
+    count = len(widths)
+    small = refs[0]
+    masters = refs[1 : 1 + count]
+    small_out = refs[1 + count]
+    outs = refs[2 + count : 2 + 2 * count]
+    at = 2 + 2 * count
+    outgoing = refs[at : at + count]
+    incoming = refs[at + count : at + 2 * count]
+    piece = refs[at + 2 * count : at + 3 * count]
+    small_send, small_recv, send, recv, local = refs[at + 3 * count :]
+    z, y, k, c = place()
+    me = (z * 4 + y * 2 + k) * 2 + c
+    barrier = greet_all()
+    for m in range(count):
+        n = widths[m]
+        left, right = masters[m][:, :n], masters[m][:, n:]
+        other = jnp.where(c == 0, right, left)
+        outgoing[m][...] = jnp.concatenate([other, jnp.zeros((8, n), F32)], 0).astype(BF16)
+    pl.semaphore_wait(barrier, 31)
+
+    def small_copy(step):
+        other = lax.rem(me + step, 32)
+        return remote(
+            small, small_out.at[me], small_send.at[step], small_recv.at[step], (other // 2, lax.rem(other, 2))
+        )
+
+    def spread(step, carry):
+        small_copy(step).start()
+        return carry
+
+    across, beside, twin = device(z, y, k, 1 - c), device(z, 1 - y, k, c), device(z, y, 1 - k, c)
+
+    def copy(m, at, src, dst, target):
+        return remote(src, dst, send.at[m, at], recv.at[m, at], target)
+
+    def pair_copy(m):
+        return copy(m, 0, outgoing[m], incoming[m], across)
+
+    def own_copy(m):
+        return pltpu.make_async_copy(piece[m], outs[m].at[c, z, y, k], local.at[m])
+
+    def line_copy(m, step):
+        return copy(m, step, piece[m], outs[m].at[c, z, y, k], device(lax.rem(z + step, 4), y, k, c))
+
+    def same(m, at, where, target):
+        view = outs[m].at[where]
+        return copy(m, at, view, view, target)
+
+    low, high = pl.ds(0, 2), pl.ds(2, 2)
+
+    def second(m):
+        return [same(m, 4, (c, low, y, k), across), same(m, 5, (c, high, y, k), beside)]
+
+    def third_own(m):
+        return [same(m, 6, (c, low, y, k), beside), same(m, 7, (c, high, y, k), across)]
+
+    def third_far(m):
+        return [same(m, 8, (1 - c, low, y, k), beside), same(m, 9, (c, high, 1 - y, k), across)]
+
+    def twin_own(m):
+        return [same(m, 10, (c, slice(None), y, k), twin)]
+
+    def twin_second(m):
+        return [same(m, 11, (1 - c, low, y, k), twin), same(m, 12, (c, high, 1 - y, k), twin)]
+
+    def twin_third(m):
+        return [
+            same(m, 13, (c, low, 1 - y, k), twin),
+            same(m, 14, (1 - c, high, y, k), twin),
+            same(m, 15, (1 - c, low, 1 - y, k), twin),
+            same(m, 16, (1 - c, high, 1 - y, k), twin),
+        ]
+
+    for m in range(count):
+        pair_copy(m).start()
+    lax.fori_loop(1, 32, spread, 0)
+    small_out[me] = small[...]
+
+    def stage_line(m):
+        n = widths[m]
+        pair_copy(m).wait_recv()
+        mine = jnp.where(c == 0, masters[m][:, :n], masters[m][:, n:])
+        theirs = incoming[m][...].astype(F32)[:24]
+        top = jnp.where(c == 0, mine, theirs)
+        bottom = jnp.where(c == 0, theirs, mine)
+        piece[m][...] = jnp.concatenate([top, bottom], 0).astype(BF16)
+        own_copy(m).start()
+        for step in (1, 3, 2):
+            line_copy(m, step).start()
+
+    def stage_second(m):
+        own_copy(m).wait()
+        for step in (1, 3, 2):
+            line_copy(m, step).wait_recv()
+        for item in second(m) + third_own(m) + twin_own(m):
+            item.start()
+
+    def stage_third(m):
+        for item in second(m):
+            item.wait_recv()
+        for item in third_far(m) + twin_second(m):
+            item.start()
+
+    def stage_twin(m):
+        for item in third_own(m) + third_far(m):
+            item.wait_recv()
+        for item in twin_third(m):
+            item.start()
+
+    def stage_end(m):
+        for item in twin_own(m) + twin_second(m) + twin_third(m):
+            item.wait_recv()
+
+    stages = (stage_line, stage_second, stage_third, stage_twin, stage_end)
+    for tick in range(count + len(stages) - 1):
+        for number, stage in enumerate(stages):
+            if 0 <= tick - number < count:
+                stage(tick - number)
+    for m in range(count):
+        pair_copy(m).wait_send()
+        for step in (1, 2, 3):
+            line_copy(m, step).wait_send()
+        for item in second(m) + third_own(m) + third_far(m) + twin_own(m) + twin_second(m) + twin_third(m):
+            item.wait_send()
+
+    def finish(step, carry):
+        small_copy(step).wait()
+        return carry
+
+    lax.fori_loop(1, 32, finish, 0)
+
+
+def gather_all(small, masters):
+    widths = tuple(m.shape[1] // 2 for m in masters)
+    count = len(widths)
+    anywhere = pl.BlockSpec(memory_space=pl.ANY)
+    inside = pl.BlockSpec(memory_space=pltpu.VMEM)
+    outs = pl.pallas_call(
+        functools.partial(gather_kernel, widths),
+        out_shape=[jax.ShapeDtypeStruct((32, *small.shape), small.dtype)]
+        + [jax.ShapeDtypeStruct((2, NZ, NY, 2, 48, n), BF16) for n in widths],
+        in_specs=[inside] * (1 + count),
+        out_specs=[inside] + [anywhere] * count,
+        scratch_shapes=[pltpu.VMEM((32, n), BF16) for n in widths] * 2
+        + [pltpu.VMEM((48, n), BF16) for n in widths]
+        + [
+            pltpu.SemaphoreType.DMA((32,)),
+            pltpu.SemaphoreType.DMA((32,)),
+            pltpu.SemaphoreType.DMA((count, 17)),
+            pltpu.SemaphoreType.DMA((count, 17)),
+            pltpu.SemaphoreType.DMA((count,)),
+        ],
+        compiler_params=pltpu.CompilerParams(
+            collective_id=0, has_side_effects=True, vmem_limit_bytes=48 * 2**20
+        ),
+    )(small, *masters)
+    return outs[0], outs[1:]
+
+
+def scatter_kernel(widths, *refs):
+    count = len(widths)
+    table = refs[0]
+    grads = refs[1 : 1 + count]
+    table_out = refs[1 + count]
+    outs = refs[2 + count : 2 + 2 * count]
+    scratch = refs[2 + 2 * count :]
+    acc, got_0, got_1a, got_1b, got_2a, got_2b, got_3, total, got_4 = (
+        scratch[i * count : (i + 1) * count] for i in range(9)
+    )
+    table_got, table_send, table_recv, send, recv, local = scratch[9 * count :]
+    z, y, k, c = place()
+    me = (z * 4 + y * 2 + k) * 2 + c
+    across, beside, twin = device(z, y, k, 1 - c), device(z, 1 - y, k, c), device(z, y, 1 - k, c)
+    barrier = greet_all()
+
+    def own_copy(m):
+        return pltpu.make_async_copy(grads[m].at[:, :, :, k], acc[m], local.at[m])
+
+    for m in range(count):
+        own_copy(m).start()
+    pl.semaphore_wait(barrier, 31)
+
+    def copy(m, at, src, dst, target):
+        return remote(src, dst, send.at[m, at], recv.at[m, at], target)
+
+    def twin_copy(m):
+        return copy(m, 0, grads[m].at[:, :, :, 1 - k], got_0[m], twin)
+
+    low, high = pl.ds(0, 2), pl.ds(2, 2)
+
+    def first(m):
+        return [
+            copy(m, 1, acc[m].at[:, low, 1 - y], got_1a[m], beside),
+            copy(m, 2, acc[m].at[1 - c, high], got_1b[m], across),
+        ]
+
+    def second(m):
+        return [
+            copy(m, 3, acc[m].at[1 - c, low, y], got_2a[m], across),
+            copy(m, 4, acc[m].at[c, high, 1 - y], got_2b[m], beside),
+        ]
+
+    def line(m):
+        return [
+            copy(m, 4 + step, acc[m].at[c, lax.rem(z + step, 4), y], got_3[m].at[step - 1], device(lax.rem(z + step, 4), y, k, c))
+            for step in (1, 2, 3)
+        ]
+
+    def pair(m):
+        return [copy(m, 8, total[m].at[1 - c], got_4[m], across)]
+
+    def table_copy(step, back):
+        other = lax.rem(me + step, 32)
+        target = (other // 2, lax.rem(other, 2))
+        if back:
+            return remote(
+                table_out.at[me], table_out.at[me], table_send.at[1, step], table_recv.at[1, step], target
+            )
+        return remote(
+            table.at[other], table_got.at[me], table_send.at[0, step], table_recv.at[0, step], target
+        )
+
+    def each(action):
+        def body(step, carry):
+            action(step)
+            return carry
+
+        lax.fori_loop(1, 32, body, 0)
+
+    def plus(left, right):
+        return (left.astype(F32) + right.astype(F32)).astype(BF16)
+
+    for m in range(count):
+        twin_copy(m).start()
+    each(lambda step: table_copy(step, False).start())
+
+    def stage_first(m):
+        own_copy(m).wait()
+        twin_copy(m).wait_recv()
+
+        def body(at, carry):
+            zz = at // 2
+            yy = lax.rem(at, 2)
+            for cc in range(2):
+                acc[m][cc, zz, yy] = plus(acc[m][cc, zz, yy], got_0[m][cc, zz, yy])
+            return carry
+
+        lax.fori_loop(0, NZ * NY, body, 0)
+        for item in first(m):
+            item.start()
+
+    def stage_second(m):
+        for item in first(m):
+            item.wait_recv()
+        for a in range(2):
+            for b in range(2):
+                acc[m][a, b, y] = plus(acc[m][a, b, y], got_1a[m][a, b])
+                acc[m][c, 2 + a, b] = plus(acc[m][c, 2 + a, b], got_1b[m][a, b])
+        for item in second(m):
+            item.start()
+
+    def stage_line(m):
+        for item in second(m):
+            item.wait_recv()
+        for a in range(2):
+            acc[m][c, a, y] = plus(acc[m][c, a, y], got_2a[m][a])
+            acc[m][c, 2 + a, y] = plus(acc[m][c, 2 + a, y], got_2b[m][a])
+        for item in line(m):
+            item.start()
+
+    def stage_pair(m):
+        for item in line(m):
+            item.wait_recv()
+        full = acc[m][c, z, y].astype(F32)
+        for step in range(3):
+            full = full + got_3[m][step].astype(F32)
+        total[m][0] = full[:24]
+        total[m][1] = full[24:]
+        for item in pair(m):
+            item.start()
+
+    def stage_end(m):
+        outs[m][c] = total[m][c]
+        for item in pair(m):
+            item.wait_recv()
+        outs[m][1 - c] = got_4[m][...]
+
+    def table_sum():
+        table_got[me] = table[me]
+        each(lambda step: table_copy(step, False).wait_recv())
+
+        def body(at, held):
+            return held + table_got[at]
+
+        table_out[me] = lax.fori_loop(1, 32, body, table_got[0])
+        each(lambda step: table_copy(step, True).start())
+
+    stages = (stage_first, stage_second, stage_line, stage_pair, stage_end)
+    for tick in range(count + len(stages) - 1):
+        for number, stage in enumerate(stages):
+            if 0 <= tick - number < count:
+                stage(tick - number)
+        if tick == count - 1:
+            table_sum()
+    each(lambda step: table_copy(step, True).wait())
+    each(lambda step: table_copy(step, False).wait_send())
+    for m in range(count):
+        for item in [twin_copy(m)] + first(m) + second(m) + line(m) + pair(m):
+            item.wait_send()
+
+
+def scatter_all(table, grads):
+    widths = tuple(g.shape[-1] for g in grads)
+    count = len(widths)
+    anywhere = pl.BlockSpec(memory_space=pl.ANY)
+    inside = pl.BlockSpec(memory_space=pltpu.VMEM)
+
+    def shapes(lead, dtype):
+        return [pltpu.VMEM((*lead, n), dtype) for n in widths]
+
+    outs = pl.pallas_call(
+        functools.partial(scatter_kernel, widths),
+        out_shape=[jax.ShapeDtypeStruct(table.shape, F32)]
+        + [jax.ShapeDtypeStruct((2, 24, n), F32) for n in widths],
+        in_specs=[inside] + [anywhere] * count,
+        out_specs=[inside] * (1 + count),
+        scratch_shapes=shapes((2, NZ, NY, 48), BF16)
+        + shapes((2, NZ, NY, 48), BF16)
+        + shapes((2, 2, 48), BF16)
+        + shapes((2, 2, 48), BF16)
+        + shapes((2, 48), BF16)
+        + shapes((2, 48), BF16)
+        + shapes((3, 48), BF16)
+        + shapes((2, 24), F32)
+        + shapes((24,), F32)
+        + [
+            pltpu.VMEM(table.shape, F32),
+            pltpu.SemaphoreType.DMA((2, 32)),
+            pltpu.SemaphoreType.DMA((2, 32)),
+            pltpu.SemaphoreType.DMA((count, 9)),
+            pltpu.SemaphoreType.DMA((count, 9)),
+            pltpu.SemaphoreType.DMA((count,)),
+        ],
+        compiler_params=pltpu.CompilerParams(
+            collective_id=1, has_side_effects=True, vmem_limit_bytes=56 * 2**20
+        ),
+    )(table, *grads)
+    return outs[0], outs[1:]
+
+
 def adam_update(master, first, second, grad_part, rate):
     first = BETA_ONE * first + (1.0 - BETA_ONE) * grad_part
     second = BETA_TWO * second + (1.0 - BETA_TWO) * grad_part * grad_part
@@ -286,12 +677,49 @@
     base = (me % per) * cw
     shard = D // ndev
 
+    tiled = lax.axis_size("seq") == 16 and ncol == 2
     inputs = jnp.where(masked > 0, MASK_ID, tokens)
-    whole = jnp.stack([inputs, targets])
-    whole = lax.all_gather(lax.all_gather(whole, "col", axis=3, tiled=True), "seq", axis=2, tiled=True)
-    pairs_all = lax.all_gather(
-        jnp.concatenate([contact_pairs, labels[:, :, None]], -1), both, axis=1, tiled=True
-    )
+    masters = [
+        jnp.concatenate(
+            [
+                jnp.pad(embedding_master.T, ((0, 0), (0, 128 - VOCAB))),
+                jnp.pad(norm_params_master.T, ((0, 0), (0, 120))),
+            ],
+            1,
+        ),
+        attention_in_master[0],
+        attention_out_master[0],
+        attention_in_master[1],
+        attention_out_master[1],
+        feed_up_master,
+        feed_down_master.T,
+    ]
+    if tiled:
+        small = jnp.concatenate(
+            [
+                inputs.reshape(4, 128),
+                targets.reshape(4, 128),
+                contact_pairs[..., 0].reshape(1, 128),
+                contact_pairs[..., 1].reshape(1, 128),
+                labels.reshape(1, 128),
+                jnp.zeros((5, 128), jnp.int32),
+            ]
+        )
+        small_all, gathered = gather_all(small, masters)
+        small_all = small_all.reshape(16, 2, 16, 128)
+        whole = small_all[:, :, :8].reshape(16, 2, 2, 2, 2, 128).transpose(2, 3, 0, 1, 4, 5).reshape(2, 2, 16, 512)
+        pairs_all = small_all[:, :, 8:11].reshape(32, 3, 2, 64).transpose(2, 0, 3, 1).reshape(2, 2048, 3)
+        gathered = [g.reshape(2, D, g.shape[-1]) for g in gathered]
+    else:
+        whole = jnp.stack([inputs, targets])
+        whole = lax.all_gather(lax.all_gather(whole, "col", axis=3, tiled=True), "seq", axis=2, tiled=True)
+        pairs_all = lax.all_gather(
+            jnp.concatenate([contact_pairs, labels[:, :, None]], -1), both, axis=1, tiled=True
+        )
+        gathered = []
+        for master in masters:
+            full = lax.all_gather(master.astype(BF16), both, axis=0, tiled=True)
+            gathered.append(full.reshape(D, 2, -1).transpose(1, 0, 2))
     counts = (
         jnp.sum(whole[0] == MASK_ID).astype(F32),
         jnp.sum(pairs_all[..., 2] >= 0).astype(F32),
@@ -303,25 +731,12 @@
     )
     pairs = lax.dynamic_index_in_dim(pairs_all, mine, 0, False)
 
-    flat = jnp.concatenate(
-        [
-            attention_in_master[0],
-            attention_in_master[1],
-            attention_out_master[0],
-            attention_out_master[1],
-            feed_up_master,
-            feed_down_master.T,
-            jnp.pad(embedding_master.T, ((0, 0), (0, VP - VOCAB))),
-            jnp.pad(norm_params_master.T, ((0, 0), (0, VP - 8))),
-        ],
-        1,
-    ).astype(BF16)
-    full = lax.all_gather(flat, both, axis=0, tiled=True)
-    edges = [0, 3 * D, 6 * D, 7 * D, 8 * D, 8 * D + FF, 8 * D + 2 * FF]
-    big = [full[:, a:b] for a, b in zip(edges[:-1], edges[1:])]
-    in_row = big[0]
-    table = full[:, edges[-1] : edges[-1] + VP].T
-    norms = full[:, edges[-1] + VP : edges[-1] + VP + 8].T.astype(F32)
+    table = gathered[0][0][:, :VP].T
+    norms = gathered[0][1][:, :8].T.astype(F32)
+    in_row, out_row, in_col, out_col, up_w, down_t = (
+        jnp.concatenate([g[0], g[1]], 1) for g in gathered[1:]
+    )
+    big = (in_row, in_col, out_row, out_col, up_w, down_t)
 
     grads, tables, contact_total, mlm_total, bce_total, kept = step(
         big,
@@ -338,10 +753,34 @@
         counts,
         cw,
     )
-    flat_grad = jnp.concatenate([g.astype(BF16) for g in grads], 1)
-    reduced = lax.psum_scatter(flat_grad, both, scatter_dimension=0, tiled=True).astype(F32)
-    table_pair, value_grad, table_grad, vectors, contact_grad, mlm_total, bce_total = lax.psum(
-        (*tables, contact_total, mlm_total, bce_total), both
+    table_pair, value_grad, table_grad, vectors = tables
+    extras = jnp.zeros((2, D), F32).at[0, : HEADS + 3].set(
+        jnp.concatenate([contact_total, mlm_total[None], bce_total[None]])
+    )
+    sums = jnp.concatenate([table_pair[:40], value_grad[:40], table_grad[:40], vectors, extras])
+    if tiled:
+        sums = sums.reshape(16, 8, 2, 384).transpose(0, 2, 1, 3).reshape(32, 8, 384)
+        blocks = []
+        for g in (grads[4], grads[3], grads[2], grads[0], grads[1]):
+            n = g.shape[1] // 2
+            blocks.append(jnp.stack([g[:, :n], g[:, n:]]).astype(BF16).reshape(2, NZ, NY, 2, 48, n))
+        sums, reduced = scatter_all(sums, blocks)
+        sums = sums.reshape(16, 2, 8, 384).transpose(0, 2, 1, 3).reshape(128, D)
+        g_down, g_up, g_out_col, g_in_col, g_out_row = (jnp.concatenate([r[0], r[1]], 1) for r in reduced)
+    else:
+        flat_grad = jnp.concatenate([g.astype(BF16) for g in grads], 1)
+        reduced = lax.psum_scatter(flat_grad, both, scatter_dimension=0, tiled=True).astype(F32)
+        g_in_col, g_out_row, g_out_col, g_up, g_down = jnp.split(
+            reduced, [3 * D, 4 * D, 5 * D, 5 * D + FF], 1
+        )
+        sums = lax.psum(sums, both)
+    spare = ((0, VP - 40), (0, 0))
+    table_pair, value_grad, table_grad = (
+        jnp.pad(sums[a : a + 40], spare) for a in (0, 40, 80)
+    )
+    vectors = sums[120:126]
+    contact_grad, mlm_total, bce_total = (
+        sums[126, : HEADS + 1], sums[126, HEADS + 1], sums[126, HEADS + 2]
     )
     unit_t, rstd_t, normed_t, query_t, key_t = kept
     row_scale = (HD * ids_all.shape[0]) ** (-0.5)
@@ -369,11 +808,10 @@
     norm_grad = jnp.concatenate([scale_0[None], vectors[:3], shift_0[None], vectors[3:]])
     table_mine = lax.dynamic_slice_in_dim(table_grad[:VOCAB], low, shard, 1)
     norm_mine = lax.dynamic_slice_in_dim(norm_grad, low, shard, 1)
-    cuts = [3 * D, 4 * D, 5 * D, 5 * D + FF]
-    g_in_col, g_out_row, g_out_col, g_up, g_down = jnp.split(reduced, cuts, 1)
+    reduced_all = (g_in_col, g_out_row, g_out_col, g_up, g_down)
 
     local_square = (
-        jnp.sum(reduced * reduced)
+        sum(jnp.sum(g * g) for g in reduced_all)
         + jnp.sum(grad_in_row * grad_in_row)
         + jnp.sum(table_mine * table_mine)
         + jnp.sum(norm_mine * norm_mine)

time: 772 us -> 569 us (0.74)
  waiting for transfers between devices: 239 us -> 0 us
  Pallas kernels: 0 us -> 213 us
  blocking collectives: 213 us -> 39.4 us
  matrix products: 161 us -> 116 us
  local copies, waits for them, and re-layouts: 76.1 us -> 119 us
  between operations: 23.6 us -> 13 us
  other arithmetic: 47.6 us -> 57.9 us
    pallas_call x0 -> x2, Pallas kernels: none -> 213 us  [the longest x1 111 us: gather_all(): pl.pallas_call(functools.partial(gather_kernel, widths), out_shape=[jax.S...]
    reduce_scatter x1 -> x0, waiting for transfers between devices: 149 us -> none  [shards(): lax.psum_scatter(flat_grad, both, scatter_dimension=0, tiled=True)]
    all_gather x3 -> x0, blocking collectives: 132 us -> none  [the longest x1 104 us: shards(): lax.all_gather(jnp.concatenate([contact_pairs, labels[:, :, None]], -1),...]
    psum x1 -> x0, waiting for transfers between devices: 77.2 us -> none  [shards(): lax.psum((*tables, contact_total, mlm_total, bce_total), both)]
    psum x1 -> x0, blocking collectives: 40.6 us -> none  [shards(): lax.psum((*tables, contact_total, mlm_total, bce_total), both)]
    dot_general x24, matrix products: 51.4 us -> 35.3 us  [tn(): lax.dot_general(left, right, (((0,), (0,)), ((), ())), preferred_element_...]
    unnamed x302 -> x268, local copies, waits for them, and re-layouts: 7.1 us -> 22.3 us
    slice x0 -> x17, local copies, waits for them, and re-layouts: none -> 14.4 us  [the longest x3 6.55 us: shards(): g[0]]
  transfers between devices with their start and end apart: 3 -> 0, of which waited for: 3 -> 0; matrix products, arithmetic and copies ran while one was open for 6% -> 0% of each run, Pallas kernels for 0% -> 0%
where the time goes in v2:
time: 569 us; the launch traced here: 559 us
  Pallas kernels  213 us (37%)
  local copies, waits for them, and re-layouts  119 us (21%)
  matrix products  116 us (20%)
  other arithmetic  57.9 us (10%)
  blocking collectives  39.4 us (7%)
  between operations  13 us (2%)
    pallas_call x1, Pallas kernels, gather_all(): pl.pallas_call(functools.partial(gather_kernel, widths), out_shape=[jax.S...  111 us
    pallas_call x1, Pallas kernels, scatter_all(): pl.pallas_call(functools.partial(scatter_kernel, widths), out_shape=[jax....  102 us
    psum x1, blocking collectives, shards(): square = lax.psum(local_square, both) + jnp.sum(contact_grad * contact_grad)  39.4 us
    dot_general x42, matrix products, nn(): lax.dot_general(left, right, (((1,), (0,)), ((), ())), preferred_element_...  37 us
    dot_general x24, matrix products, tn(): lax.dot_general(left, right, (((0,), (0,)), ((), ())), preferred_element_...  35.3 us
    dot_general x35, matrix products, nt(): lax.dot_general(left, right, (((1,), (1,)), ((), ())), preferred_element_...  32.6 us
    unnamed x268, local copies, waits for them, and re-layouts  22.3 us
    reshape x6, local copies, waits for them, and re-layouts, to_heads(): block.reshape(rows, cw, HEADS, VP).transpose(2, 1, 0, 3)  15.2 us

profile of v2, /device:TPU:0, one launch (start us, length us, event | category | flops | bytes accessed | tf_op | source)
XLA Modules:
  0.0 558.5 jit_solution(10819146790355386000)
XLA Ops:
  11.8 110.7 %shard_map.465 = (s32[32,16,128]{2,1,0:T(8,128)S(1)}, bf16[2,4,2,2,48,128]{5,4,3,2,1,0:T(8,128)(2,1)S(1)}, bf16[2,4,2,2,48,1152]{5,4,3,2,1,0:T(8,128)(2,1)}, bf1...) custom-call(s32[16,128]{1,0:T(8,128)S(1)} %concatenate.90.refs_0_, ...), custom_call_target="tpu_custom_call" | custom-call | tf_op jit(solution)/shard_map/pallas_call | solution.py:420
  136.0 4.4 fusion.419
  147.0 2.7 reshape.689
  151.9 2.8 reshape.690
  156.2 2.7 reshape.691
  161.1 3.0 reshape.692
  176.5 4.3 copy.252
  180.8 3.8 reshape.693
  201.4 2.4 reshape.695
  206.1 2.4 reshape.696
  210.8 2.6 reshape.694
  224.0 2.7 fusion.8
  226.8 3.8 fusion.435
  239.9 2.4 multiply_reduce_fusion.1
  245.4 8.2 %multiply_convert_fusion = bf16[512,3072]{1,0:T(8,128)(2,1)S(1)} fusion(f32[512,3072]{1,0:T(8,128)} %copy-done.121, bf16[768,1536]{1,0:T(8,128)(2,1)S(1)} %bitcast.330, bf16[768,1536]{1,0:T(8,128)(2,1)S(1)} %bitcast.332, f32[512,768]{1,0:T(8,128)S(1)} %subtract_multiply_fusion), kind=kOutput, calls=%fused_computation.1 | convolution fusion | flops 2454061056 | bytes 15728640 | tf_op jit(solution)/shard_map/dot_general | solution.py:33
  253.6 3.0 multiply_reduce_fusion.2
  256.7 3.2 convolution_convert_fusion.2
  260.8 2.5 pad_maximum_fusion.2.refs_1_
  266.3 4.9 convolution_convert_fusion.1
  273.5 2.8 reshape.698
  276.4 2.7 fusion.414
  279.1 2.6 pad_maximum_fusion.3.refs_2_
  295.5 2.6 multiply_reduce_fusion.3
  300.2 4.3 convolution_convert_fusion
  304.5 3.0 convolution_convert_fusion.13
  341.9 2.6 concatenate.103
  344.4 5.5 fusion.14
  352.9 2.6 copy.276
  366.4 3.5 concatenate.106
  369.9 102.3 %shard_map.466 = (f32[32,8,384]{2,1,0:T(8,128)}, f32[2,24,1536]{2,1,0:T(8,128)}, f32[2,24,1536]{2,1,0:T(8,128)}, f32[2,24,384]{2,1,0:T(8,128)}, f32[2,24,1152]{2,1,0:T(8,128)}, /*index=5*/f32[2,24,384]{2,1,0:T(8,128)}) custom-call(f32[32,8,384]{2,1,0:T(8,128)} %bitcast.349, bf16[2,4,2,2,48,1536]{5,4,3,2,1,0:T(8,128)(2,1)} %pad_maximum_fusion.2.refs_1_, ...), custom_call_target="tpu_custom_call" | custom-call | tf_op jit(solution)/shard_map/pallas_call | solution.py:603
  498.6 2.8 fusion.49
  507.4 39.4 %psum.7 = f32[]{:T(128)} all-reduce(f32[]{:T(128)S(6)} %add.436), channel_id=1, replica_groups=mesh['seq'=16,'col'=2] {'seq','col'}, use_global_device_ids=true, to_apply=%region_50.51 | all-reduce | flops 1 | bytes 8 | tf_op jit(solution)/shard_map/psum | solution.py:819
  (555 shorter events, 196.1 us)
Async XLA Ops:
  0.7 11.1 %copy-start = (f32[3072,24]{0,1:T(8,128)S(1)}, f32[3072,24]{0,1:T(8,128)}, u32[]{:S(2)}) copy-start(f32[3072,24]{0,1:T(8,128)} %param.42) | copy-start | bytes 884740
  0.7 11.1 %copy-start.1 = (f32[24,3072]{1,0:T(8,128)S(1)}, f32[24,3072]{1,0:T(8,128)}, u32[]{:S(2)}) copy-start(f32[24,3072]{1,0:T(8,128)} %refs_6_.1) | copy-start | bytes 884740
  6.8 183.9 %copy-start.90 = (s32[512]{0:T(512)}, s32[512]{0:T(512)S(1)}, u32[]{:S(2)}) copy-start(s32[512]{0:T(512)S(1)} %get-tuple-element.339) | copy-start | bytes 6148
  6.8 183.9 %copy-start.92 = (s32[512]{0:T(512)}, s32[512]{0:T(512)S(1)}, u32[]{:S(2)}) copy-start(s32[512]{0:T(512)S(1)} %get-tuple-element.340) | copy-start | bytes 6148
  124.5 7.5 %copy-start.104 = (f32[64]{0:T(128)}, f32[64]{0:T(128)S(1)}, u32[]{:S(2)}) copy-start(f32[64]{0:T(128)S(1)} %add_rsqrt_fusion.3) | copy-start | bytes 772
  131.2 9.2 %copy-start.71 = (bf16[64,768]{0,1:T(8,128)(2,1)}, bf16[64,768]{0,1:T(8,128)(2,1)S(1)}, u32[]{:S(2)}) copy-start(bf16[64,768]{0,1:T(8,128)(2,1)S(1)} %add_convert_fusion.5) | copy-start | bytes 294916
  193.4 25.2 %copy-start.2 = (f32[512,768]{1,0:T(8,128)}, f32[512,768]{1,0:T(8,128)S(1)}, u32[]{:S(2)}) copy-start(f32[512,768]{1,0:T(8,128)S(1)} %get-tuple-element.319) | copy-start | bytes 4718596
  243.0 13.7 %slice-start.5 = ((s8[6291456]{0:T(1024)(128)(4,1)}), s8[2097152]{0:T(1024)(128)(4,1)S(1)}, s32[]{:S(2)}) async-start(s8[6291456]{0:T(1024)(128)(4,1)} %bitcast.397), calls=%async_computation.5 | async-start | bytes 4194304
  245.3 8.2 %copy-start.10 = (f32[512,768]{1,0:T(8,128)S(1)}, f32[512,768]{1,0:T(8,128)}, u32[]{:S(2)}) copy-start(f32[512,768]{1,0:T(8,128)} %copy-done.9) | copy-start | bytes 4718596
  245.3 8.2 %copy-start.18 = (bf16[1,4,2,2,48,1536]{5,4,3,2,1,0:T(8,128)(2,1)S(1)}, bf16[1,4,2,2,48,1536]{5,4,3,2,1,0:T(8,128)(2,1)}, u32[]{:S(2)}) copy-start(bf16[1,4,2,2,48,1536]{5,4,3,2,1,0:T(8,128)(2,1)} %copy-done.17) | copy-start | bytes 7077892
  245.4 8.3 %copy-start.20 = (bf16[1,4,2,2,48,1536]{5,4,3,2,1,0:T(8,128)(2,1)S(1)}, bf16[1,4,2,2,48,1536]{5,4,3,2,1,0:T(8,128)(2,1)}, u32[]{:S(2)}) copy-start(bf16[1,4,2,2,48,1536]{5,4,3,2,1,0:T(8,128)(2,1)} %copy-done.19) | copy-start | bytes 7077892
  245.4 8.3 %copy-start.99 = (f32[512]{0:T(512)S(1)}, f32[512]{0:T(512)}, u32[]{:S(2)}) copy-start(f32[512]{0:T(512)} %copy-done.98) | copy-start | bytes 6148
  245.4 11.3 %slice-start.6 = ((s8[6291456]{0:T(1024)(128)(4,1)}), s8[4194304]{0:T(1024)(128)(4,1)S(1)}, s32[]{:S(2)}) async-start(s8[6291456]{0:T(1024)(128)(4,1)} %bitcast.397), calls=%async_computation.6 | async-start | bytes 8388608
  472.2 8.9 %copy-start.68 = (f32[2,24,1536]{2,1,0:T(8,128)S(1)}, f32[2,24,1536]{2,1,0:T(8,128)}, u32[]{:S(2)}) copy-start(f32[2,24,1536]{2,1,0:T(8,128)} %get-tuple-element.66) | copy-start | bytes 884740
  472.2 10.3 %copy-start.67 = (f32[2,24,1536]{2,1,0:T(8,128)S(1)}, f32[2,24,1536]{2,1,0:T(8,128)}, u32[]{:S(2)}) copy-start(f32[2,24,1536]{2,1,0:T(8,128)} %get-tuple-element.67) | copy-start | bytes 884740
  481.1 7.3 %copy-start.34 = (f32[24,1536]{1,0:T(8,128)}, f32[24,1536]{1,0:T(8,128)S(1)}, u32[]{:S(2)}) copy-start(f32[24,1536]{1,0:T(8,128)S(1)} %get-tuple-element.292) | copy-start | bytes 442372
  484.0 7.7 %copy-start.60 = (f32[16,8,2,384]{3,1,2,0:T(8,128)}, f32[16,8,2,384]{3,1,2,0:T(8,128)S(1)}, u32[]{:S(2)}) copy-start(f32[16,8,2,384]{3,1,2,0:T(8,128)S(1)} %copy.304) | copy-start | bytes 1179652
  501.5 46.7 %copy-start.117 = (f32[13]{0:T(128)S(1)}, f32[13]{0:T(128)}, u32[]{:S(2)}) copy-start(f32[13]{0:T(128)} %param.51) | copy-start | bytes 160
  501.6 46.7 %copy-start.118 = (f32[13]{0:T(128)S(1)}, f32[13]{0:T(128)}, u32[]{:S(2)}) copy-start(f32[13]{0:T(128)} %param.52) | copy-start | bytes 160
  501.6 46.7 %copy-start.119 = (f32[13]{0:T(128)S(1)}, f32[13]{0:T(128)}, u32[]{:S(2)}) copy-start(f32[13]{0:T(128)} %param.53) | copy-start | bytes 160
  501.6 47.9 %copy-start.82 = (f32[8,24]{1,0:T(8,128)S(1)}, f32[8,24]{1,0:T(8,128)}, u32[]{:S(2)}) copy-start(f32[8,24]{1,0:T(8,128)} %param.48) | copy-start | bytes 2308
  501.6 47.9 %copy-start.112 = (f32[8,24]{1,0:T(8,128)S(1)}, f32[8,24]{1,0:T(8,128)}, u32[]{:S(2)}) copy-start(f32[8,24]{1,0:T(8,128)} %param.49) | copy-start | bytes 2308
  501.6 47.9 %copy-start.113 = (f32[8,24]{1,0:T(8,128)S(1)}, f32[8,24]{1,0:T(8,128)}, u32[]{:S(2)}) copy-start(f32[8,24]{1,0:T(8,128)} %param.50) | copy-start | bytes 2308
  501.6 48.5 %copy-start.77 = (f32[33,24]{0,1:T(8,128)S(1)}, f32[33,24]{0,1:T(8,128)}, u32[]{:S(2)}) copy-start(f32[33,24]{0,1:T(8,128)} %param.45) | copy-start | bytes 9508
  501.6 48.5 %copy-start.88 = (f32[33,24]{0,1:T(8,128)S(1)}, f32[33,24]{0,1:T(8,128)}, u32[]{:S(2)}) copy-start(f32[33,24]{0,1:T(8,128)} %param.46) | copy-start | bytes 9508
  501.6 48.5 %copy-start.89 = (f32[33,24]{0,1:T(8,128)S(1)}, f32[33,24]{0,1:T(8,128)}, u32[]{:S(2)}) copy-start(f32[33,24]{0,1:T(8,128)} %param.47) | copy-start | bytes 9508
  501.6 49.1 %copy-start.55 = (f32[2,24,768]{2,1,0:T(8,128)S(1)}, f32[2,24,768]{2,1,0:T(8,128)}, u32[]{:S(2)}) copy-start(f32[2,24,768]{2,1,0:T(8,128)} %param.36) | copy-start | bytes 442372
  501.7 49.1 %copy-start.69 = (f32[1,24,768]{2,1,0:T(8,128)S(1)}, f32[1,24,768]{2,1,0:T(8,128)}, u32[]{:S(2)}) copy-start(f32[1,24,768]{2,1,0:T(8,128)} %get-tuple-element.304) | copy-start | bytes 221188
  503.9 48.8 %copy-start.37 = (f32[24,1536]{1,0:T(8,128)S(1)}, f32[24,1536]{1,0:T(8,128)}, u32[]{:S(2)}) copy-start(f32[24,1536]{1,0:T(8,128)} %copy-done.36) | copy-start | bytes 442372
  503.9 48.8 %copy-start.39 = (f32[24,1536]{1,0:T(8,128)S(1)}, f32[24,1536]{1,0:T(8,128)}, u32[]{:S(2)}) copy-start(f32[24,1536]{1,0:T(8,128)} %copy-done.38) | copy-start | bytes 442372
  503.9 48.8 %copy-start.63 = (f32[3072,24]{0,1:T(8,128)S(1)}, f32[3072,24]{0,1:T(8,128)}, u32[]{:S(2)}) copy-start(f32[3072,24]{0,1:T(8,128)} %param.43) | copy-start | bytes 884740
  503.9 48.8 %copy-start.64 = (f32[3072,24]{0,1:T(8,128)S(1)}, f32[3072,24]{0,1:T(8,128)}, u32[]{:S(2)}) copy-start(f32[3072,24]{0,1:T(8,128)} %param.44) | copy-start | bytes 884740
  (97 other events, 264.8 us)
